TPU v7x, 32 devices: a whole 2x2x4 slice. The times are simulated.
32 devices in a mesh: leaf: 8 (over z, x), sub: 4 (over y, core).
Axes of the slice: x: 2, y: 2, z: 4, core: 2. Of those that a mesh axis runs over, the one named last changes fastest.
Arguments:
- coords: bfloat16 [4096, 3, 128], P('leaf'), may hold values from 0 to 4
- charges: bfloat16 [4096, 8, 128], P(('leaf', 'sub')), may hold values from -6 to 6
- counts: int32 [4096], P('leaf'), may hold values from 32 to 128, as said below
- morton: int32 [4096], P('leaf'), may hold values from 0 to 511, as said below
- near_list: int32 [4096, 27], P(('leaf', 'sub')), may hold values from -1 to 4095, as said below
- basis: bfloat16 [4096, 64, 128], P(('leaf', 'sub')), may hold values from -0.5 to 0.5
- transfer1: bfloat16 [4096, 64, 64], P(('leaf', 'sub')), may hold values from -0.75 to 0.75
- far2_list: int32 [512, 16], P(('leaf', 'sub')), may hold values from -1 to 511, as said below
- coupling2: bfloat16 [512, 16, 64, 64], P(('leaf', 'sub')), may hold values from -0.0625 to 0.0625
- transfer2: bfloat16 [512, 64, 64], P('leaf'), may hold values from -0.75 to 0.75
- far3_list: int32 [8, 8], P('leaf'), may hold values from -1 to 7, as said below
- coupling3: bfloat16 [8, 8, 64, 64], P('leaf'), may hold values from -0.01171875 to 0.01171875
Outputs:
- potential: float32 [4096, 8, 128], P(('leaf', 'sub'))
Inputs may be any that keep to these rules, and one draw needn't show every extreme that they name: `counts`: each leaf's number of live points; leaves do not all have the same number. `morton`: within every block of 512 consecutive entries, a permutation of 0 to 511. `near_list`: row t starts with t itself; its other live entries are leaves other than t in the leaf group of t or in the group just before or after it; live entries come first and -1 fills the rest, with at least 13 live entries a row; entries may repeat. `far2_list`: row b names boxes other than b in the leaf group of b or in the group just before or after it; live entries come first and -1 fills the rest, with at least 8 live entries a row; entries may repeat. `far3_list`: row q names group boxes other than q; live entries come first and -1 fills the rest, with at least 4 live entries a row; entries may repeat.
All inputs are finite; a program needn't handle non-finite values.
Results may differ from a plain program's by a relative error of at most 0.011.
Values may be sent and summed in bfloat16 or wider, within the bound.
A program may use at most 64 MiB of HBM per device.

v0:
```python
import jax
import jax.numpy as jnp
from jax import lax
from jax.sharding import PartitionSpec as P

kernel_scale = 0.07957747154594767
delta_squared = 0.0025


def with_halo(cells, sides, width):
    for axis, dim in sides:
        count = lax.axis_size(axis)
        ends = count - 1
        head = lax.slice_in_dim(cells, 0, width, axis=dim)
        tail = lax.slice_in_dim(cells, cells.shape[dim] - width, cells.shape[dim], axis=dim)
        cells = jnp.concatenate(
            [
                lax.ppermute(tail, axis, [(i, (i + 1) % count) for i in range(ends)]),
                cells,
                lax.ppermute(head, axis, [((i + 1) % count, i) for i in range(ends)]),
            ],
            axis=dim,
        )
    return cells


def kernel_tile(targets, sources):
    squared = jnp.zeros((targets.shape[0], targets.shape[2], sources.shape[2]), jnp.float32)
    for component in range(3):
        offset = targets[:, component, :, None] - sources[:, component, None, :]
        squared = squared + offset * offset
    return (kernel_scale / jnp.sqrt(squared + delta_squared)).astype(jnp.bfloat16)


def far_field(moments, lists, couplings, offset):
    valid = lists >= 0
    local = jnp.clip(lists - offset, 0, moments.shape[0] - 1)
    source = jnp.where(valid[..., None, None], moments[local], jnp.zeros((), moments.dtype))
    return jnp.einsum("bkrc,bkcp->brp", source, couplings, preferred_element_type=jnp.float32)


def on_device(
    coords,
    charges,
    counts,
    morton,
    near_list,
    basis,
    transfer1,
    far2_list,
    coupling2,
    transfer2,
    far3_list,
    coupling3,
):
    lane = lax.axis_index("sub")
    group = lax.axis_index("leaf")
    leaf_dev = charges.shape[0]
    rhs_count = charges.shape[1]
    points = charges.shape[2]
    rank_size = basis.shape[1]
    group_size = coords.shape[0]
    clusters = far2_list.shape[0]
    group_boxes = transfer2.shape[0]
    start = lane * leaf_dev
    arrived = lax.all_gather(charges, "sub", axis=0, tiled=True)
    inverse = (
        jnp.zeros((group_size,), jnp.int32).at[morton].set(jnp.arange(group_size, dtype=jnp.int32))
    )
    ordered = arrived[inverse]
    live = jnp.arange(points, dtype=jnp.int32)[None, :] < counts[:, None]
    masked = jnp.where(live[:, None, :], ordered, jnp.zeros((), ordered.dtype))
    packed = jnp.concatenate([coords, masked], axis=1)
    nearby = with_halo(packed, (("leaf", 0),), group_size)
    own_charges = lax.dynamic_slice_in_dim(masked, start, leaf_dev, 0)
    own_live = lax.dynamic_slice_in_dim(live, start, leaf_dev, 0)
    targets = lax.dynamic_slice_in_dim(coords, start, leaf_dev, 0).astype(jnp.float32)
    transfer_boxed = transfer1.reshape(clusters, 8, rank_size, rank_size)
    leaf_moments = jnp.einsum(
        "trp,tkp->trk", own_charges, basis, preferred_element_type=jnp.float32
    ).astype(jnp.bfloat16)
    box_moments = jnp.einsum(
        "bnrc,bncp->brp",
        leaf_moments.reshape(clusters, 8, rhs_count, rank_size),
        transfer_boxed,
        preferred_element_type=jnp.float32,
    ).astype(jnp.bfloat16)
    group_moments = lax.all_gather(box_moments, "sub", axis=0, tiled=True)
    top_moment = jnp.einsum(
        "brc,bcp->rp", group_moments, transfer2, preferred_element_type=jnp.float32
    ).astype(jnp.bfloat16)
    all_top = lax.all_gather(top_moment[None], "leaf", axis=0, tiled=True)
    near_boxes = with_halo(group_moments, (("leaf", 0),), group_boxes)
    top_field = far_field(all_top, far3_list, coupling3, 0).astype(jnp.bfloat16)
    box_far = far_field(near_boxes, far2_list, coupling2, (group - 1) * group_boxes)
    own_transfer = lax.dynamic_slice_in_dim(transfer2, lane * clusters, clusters, 0)
    box_local = (
        box_far
        + jnp.einsum("rp,bcp->brc", top_field[0], own_transfer, preferred_element_type=jnp.float32)
    ).astype(jnp.bfloat16)
    leaf_local = jnp.einsum(
        "brp,bncp->bnrc", box_local, transfer_boxed, preferred_element_type=jnp.float32
    ).astype(jnp.bfloat16)
    leaf_local = leaf_local.reshape(leaf_dev, rhs_count, rank_size)
    far_part = jnp.einsum("trk,tkp->trp", leaf_local, basis, preferred_element_type=jnp.float32)
    base = (group - 1) * group_size

    def slot_step(total, column):
        valid = column >= 0
        index = jnp.clip(column - base, 0, 3 * group_size - 1)
        rows = nearby[index]
        tile = kernel_tile(targets, rows[:, :3].astype(jnp.float32))
        source = jnp.where(valid[:, None, None], rows[:, 3:], jnp.zeros((), rows.dtype))
        return (
            total + jnp.einsum("tij,trj->tri", tile, source, preferred_element_type=jnp.float32),
            None,
        )

    near_part, unused = lax.scan(
        slot_step, jnp.zeros((leaf_dev, rhs_count, points), jnp.float32), near_list.T
    )
    return jnp.where(own_live[:, None, :], near_part + far_part, jnp.zeros((), jnp.float32))


def solution(mesh):
    return jax.shard_map(
        on_device,
        mesh=mesh,
        in_specs=(
            P("leaf", None, None),
            P(("leaf", "sub"), None, None),
            P("leaf"),
            P("leaf"),
            P(("leaf", "sub"), None),
            P(("leaf", "sub"), None, None),
            P(("leaf", "sub"), None, None),
            P(("leaf", "sub"), None),
            P(("leaf", "sub"), None, None, None),
            P("leaf", None, None),
            P("leaf", None),
            P("leaf", None, None, None),
        ),
        out_specs=P(("leaf", "sub"), None, None),
        check_vma=False,
    )
```

profile of v0, /device:TPU:10, one launch (start us, length us, event | category | flops | bytes accessed | tf_op | source)
XLA Modules:
  0.0 665.4 jit_solution(7482105814204220354)
XLA Ops:
  19.3 7.6 %all-gather.3.cloned.1.call-done = bf16[512,8,128]{2,1,0:T(8,128)(2,1)} async-done(((bf16[128,8,128]{2,1,0:T(8,128)(2,1)}), bf16[512,8,128]{2,1,0:T(8,128)(2,1)}) %all-gather.3.cloned.1.call-update) | async-done | bytes 1048592 | tf_op jit(solution)/shard_map/all_gather | solution.py:66
  42.6 5.4 all_gather.10
  54.6 71.2 %all-gather = bf16[64,64]{1,0:T(8,128)(2,1)S(1)} all-gather(bf16[8,64]{1,0:T(8,128)(2,1)S(1)} %fusion.12), channel_id=2, replica_groups=mesh['leaf'=8,'sub'=4] {'leaf'}, dimensions={0}, use_global_device_ids=true | all-gather | bytes 9216 | tf_op jit(solution)/shard_map/all_gather | solution.py:92
  147.0 25.7 %pad_maximum_fusion = bf16[1536,11,128]{2,1,0:T(8,128)(2,1)} fusion(bf16[512,11,128]{2,1,0:T(8,128)(2,1)S(1)} %copy.22, bf16[512,8,128]{2,1,0:T(8,128)(2,1)S(1)} %broadcast_select_fusion, bf16[512,3,128]{2,1,0:T(4,128)(2,1)S(1)} %copy-done.2, bf16[512,11,128]{2,1,0:T(8,128)(2,1)S(1)} %copy.21), kind=kLoop, calls=%fused_computation.23 | loop fusion | flops 17301504 | bytes 8650752 | tf_op jit(solution)/shard_map/concatenate | solution.py:16
  172.8 483.8 %while.11 = (s32[]{:T(128)}, f32[128,8,128]{2,1,0:T(8,128)}, s32[27,128]{1,0:T(8,128)}, s32[]{:T(128)}, bf16[1536,11,128]{2,1,0:T(8,128)(2,1)}, /*index=5*/f32[128,3,128]{2,0,1:T(8,128)S(1)}, s32[]{:T(128)}, s32[]{:T(128)}) while((s32[]{:T(128)}, f32[128,8,128]{2,1,0:T(8,128)}, s32[27,128]{1,0:T(8,128)}, s32[]{:T(128)}, ...), condition=%wide.region_2.3_spmd.clone, body=%wide.region_1.2_spmd.clone.sunk | while | flops 57067264 | bytes 3513195 | solution.py:119
  179.2 11.5 %fusion.50 = f32[128,8,128]{2,1,0:T(8,128)} fusion(f32[128,128]{1,0:T(8,128)S(1)} %bitcast.93, f32[128,128]{1,0:T(8,128)} %get-tuple-element.121, f32[128,128]{1,0:T(8,128)S(1)} %bitcast.94, f32[128,128]{1,0:T(8,128)} %get-tuple-element.123, f32[128,128]{1,0:T(8,128)S(1)} %bitcast.92, f32[128,128]{1,0:T(8,128)} %get-tuple-element.125, ...), kind=kOutput, calls=%fused_computation.7.clone.1 | convolution fusion | flops 57016320 | bytes 1704065 | tf_op jit(solution)/shard_map/while/body/eval_jaxpr/tij,trj->tri/dot_general | solution.py:115
  197.0 11.6 %fusion.50 = f32[128,8,128]{2,1,0:T(8,128)} fusion(f32[128,128]{1,0:T(8,128)S(1)} %bitcast.93, f32[128,128]{1,0:T(8,128)} %get-tuple-element.121, f32[128,128]{1,0:T(8,128)S(1)} %bitcast.94, f32[128,128]{1,0:T(8,128)} %get-tuple-element.123, f32[128,128]{1,0:T(8,128)S(1)} %bitcast.92, f32[128,128]{1,0:T(8,128)} %get-tuple-element.125, ...), kind=kOutput, calls=%fused_computation.7.clone.1 | convolution fusion | flops 57016320 | bytes 1704065 | tf_op jit(solution)/shard_map/while/body/eval_jaxpr/tij,trj->tri/dot_general | solution.py:115
  215.0 11.6 %fusion.50 = f32[128,8,128]{2,1,0:T(8,128)} fusion(f32[128,128]{1,0:T(8,128)S(1)} %bitcast.93, f32[128,128]{1,0:T(8,128)} %get-tuple-element.121, f32[128,128]{1,0:T(8,128)S(1)} %bitcast.94, f32[128,128]{1,0:T(8,128)} %get-tuple-element.123, f32[128,128]{1,0:T(8,128)S(1)} %bitcast.92, f32[128,128]{1,0:T(8,128)} %get-tuple-element.125, ...), kind=kOutput, calls=%fused_computation.7.clone.1 | convolution fusion | flops 57016320 | bytes 1704065 | tf_op jit(solution)/shard_map/while/body/eval_jaxpr/tij,trj->tri/dot_general | solution.py:115
  232.9 11.6 %fusion.50 = f32[128,8,128]{2,1,0:T(8,128)} fusion(f32[128,128]{1,0:T(8,128)S(1)} %bitcast.93, f32[128,128]{1,0:T(8,128)} %get-tuple-element.121, f32[128,128]{1,0:T(8,128)S(1)} %bitcast.94, f32[128,128]{1,0:T(8,128)} %get-tuple-element.123, f32[128,128]{1,0:T(8,128)S(1)} %bitcast.92, f32[128,128]{1,0:T(8,128)} %get-tuple-element.125, ...), kind=kOutput, calls=%fused_computation.7.clone.1 | convolution fusion | flops 57016320 | bytes 1704065 | tf_op jit(solution)/shard_map/while/body/eval_jaxpr/tij,trj->tri/dot_general | solution.py:115
  250.8 11.6 %fusion.50 = f32[128,8,128]{2,1,0:T(8,128)} fusion(f32[128,128]{1,0:T(8,128)S(1)} %bitcast.93, f32[128,128]{1,0:T(8,128)} %get-tuple-element.121, f32[128,128]{1,0:T(8,128)S(1)} %bitcast.94, f32[128,128]{1,0:T(8,128)} %get-tuple-element.123, f32[128,128]{1,0:T(8,128)S(1)} %bitcast.92, f32[128,128]{1,0:T(8,128)} %get-tuple-element.125, ...), kind=kOutput, calls=%fused_computation.7.clone.1 | convolution fusion | flops 57016320 | bytes 1704065 | tf_op jit(solution)/shard_map/while/body/eval_jaxpr/tij,trj->tri/dot_general | solution.py:115
  268.7 11.6 %fusion.50 = f32[128,8,128]{2,1,0:T(8,128)} fusion(f32[128,128]{1,0:T(8,128)S(1)} %bitcast.93, f32[128,128]{1,0:T(8,128)} %get-tuple-element.121, f32[128,128]{1,0:T(8,128)S(1)} %bitcast.94, f32[128,128]{1,0:T(8,128)} %get-tuple-element.123, f32[128,128]{1,0:T(8,128)S(1)} %bitcast.92, f32[128,128]{1,0:T(8,128)} %get-tuple-element.125, ...), kind=kOutput, calls=%fused_computation.7.clone.1 | convolution fusion | flops 57016320 | bytes 1704065 | tf_op jit(solution)/shard_map/while/body/eval_jaxpr/tij,trj->tri/dot_general | solution.py:115
  286.6 11.6 %fusion.50 = f32[128,8,128]{2,1,0:T(8,128)} fusion(f32[128,128]{1,0:T(8,128)S(1)} %bitcast.93, f32[128,128]{1,0:T(8,128)} %get-tuple-element.121, f32[128,128]{1,0:T(8,128)S(1)} %bitcast.94, f32[128,128]{1,0:T(8,128)} %get-tuple-element.123, f32[128,128]{1,0:T(8,128)S(1)} %bitcast.92, f32[128,128]{1,0:T(8,128)} %get-tuple-element.125, ...), kind=kOutput, calls=%fused_computation.7.clone.1 | convolution fusion | flops 57016320 | bytes 1704065 | tf_op jit(solution)/shard_map/while/body/eval_jaxpr/tij,trj->tri/dot_general | solution.py:115
  304.6 11.6 %fusion.50 = f32[128,8,128]{2,1,0:T(8,128)} fusion(f32[128,128]{1,0:T(8,128)S(1)} %bitcast.93, f32[128,128]{1,0:T(8,128)} %get-tuple-element.121, f32[128,128]{1,0:T(8,128)S(1)} %bitcast.94, f32[128,128]{1,0:T(8,128)} %get-tuple-element.123, f32[128,128]{1,0:T(8,128)S(1)} %bitcast.92, f32[128,128]{1,0:T(8,128)} %get-tuple-element.125, ...), kind=kOutput, calls=%fused_computation.7.clone.1 | convolution fusion | flops 57016320 | bytes 1704065 | tf_op jit(solution)/shard_map/while/body/eval_jaxpr/tij,trj->tri/dot_general | solution.py:115
  322.5 11.6 %fusion.50 = f32[128,8,128]{2,1,0:T(8,128)} fusion(f32[128,128]{1,0:T(8,128)S(1)} %bitcast.93, f32[128,128]{1,0:T(8,128)} %get-tuple-element.121, f32[128,128]{1,0:T(8,128)S(1)} %bitcast.94, f32[128,128]{1,0:T(8,128)} %get-tuple-element.123, f32[128,128]{1,0:T(8,128)S(1)} %bitcast.92, f32[128,128]{1,0:T(8,128)} %get-tuple-element.125, ...), kind=kOutput, calls=%fused_computation.7.clone.1 | convolution fusion | flops 57016320 | bytes 1704065 | tf_op jit(solution)/shard_map/while/body/eval_jaxpr/tij,trj->tri/dot_general | solution.py:115
  340.4 11.6 %fusion.50 = f32[128,8,128]{2,1,0:T(8,128)} fusion(f32[128,128]{1,0:T(8,128)S(1)} %bitcast.93, f32[128,128]{1,0:T(8,128)} %get-tuple-element.121, f32[128,128]{1,0:T(8,128)S(1)} %bitcast.94, f32[128,128]{1,0:T(8,128)} %get-tuple-element.123, f32[128,128]{1,0:T(8,128)S(1)} %bitcast.92, f32[128,128]{1,0:T(8,128)} %get-tuple-element.125, ...), kind=kOutput, calls=%fused_computation.7.clone.1 | convolution fusion | flops 57016320 | bytes 1704065 | tf_op jit(solution)/shard_map/while/body/eval_jaxpr/tij,trj->tri/dot_general | solution.py:115
  358.3 11.6 %fusion.50 = f32[128,8,128]{2,1,0:T(8,128)} fusion(f32[128,128]{1,0:T(8,128)S(1)} %bitcast.93, f32[128,128]{1,0:T(8,128)} %get-tuple-element.121, f32[128,128]{1,0:T(8,128)S(1)} %bitcast.94, f32[128,128]{1,0:T(8,128)} %get-tuple-element.123, f32[128,128]{1,0:T(8,128)S(1)} %bitcast.92, f32[128,128]{1,0:T(8,128)} %get-tuple-element.125, ...), kind=kOutput, calls=%fused_computation.7.clone.1 | convolution fusion | flops 57016320 | bytes 1704065 | tf_op jit(solution)/shard_map/while/body/eval_jaxpr/tij,trj->tri/dot_general | solution.py:115
  376.3 11.6 %fusion.50 = f32[128,8,128]{2,1,0:T(8,128)} fusion(f32[128,128]{1,0:T(8,128)S(1)} %bitcast.93, f32[128,128]{1,0:T(8,128)} %get-tuple-element.121, f32[128,128]{1,0:T(8,128)S(1)} %bitcast.94, f32[128,128]{1,0:T(8,128)} %get-tuple-element.123, f32[128,128]{1,0:T(8,128)S(1)} %bitcast.92, f32[128,128]{1,0:T(8,128)} %get-tuple-element.125, ...), kind=kOutput, calls=%fused_computation.7.clone.1 | convolution fusion | flops 57016320 | bytes 1704065 | tf_op jit(solution)/shard_map/while/body/eval_jaxpr/tij,trj->tri/dot_general | solution.py:115
  394.2 11.6 %fusion.50 = f32[128,8,128]{2,1,0:T(8,128)} fusion(f32[128,128]{1,0:T(8,128)S(1)} %bitcast.93, f32[128,128]{1,0:T(8,128)} %get-tuple-element.121, f32[128,128]{1,0:T(8,128)S(1)} %bitcast.94, f32[128,128]{1,0:T(8,128)} %get-tuple-element.123, f32[128,128]{1,0:T(8,128)S(1)} %bitcast.92, f32[128,128]{1,0:T(8,128)} %get-tuple-element.125, ...), kind=kOutput, calls=%fused_computation.7.clone.1 | convolution fusion | flops 57016320 | bytes 1704065 | tf_op jit(solution)/shard_map/while/body/eval_jaxpr/tij,trj->tri/dot_general | solution.py:115
  412.1 11.6 %fusion.50 = f32[128,8,128]{2,1,0:T(8,128)} fusion(f32[128,128]{1,0:T(8,128)S(1)} %bitcast.93, f32[128,128]{1,0:T(8,128)} %get-tuple-element.121, f32[128,128]{1,0:T(8,128)S(1)} %bitcast.94, f32[128,128]{1,0:T(8,128)} %get-tuple-element.123, f32[128,128]{1,0:T(8,128)S(1)} %bitcast.92, f32[128,128]{1,0:T(8,128)} %get-tuple-element.125, ...), kind=kOutput, calls=%fused_computation.7.clone.1 | convolution fusion | flops 57016320 | bytes 1704065 | tf_op jit(solution)/shard_map/while/body/eval_jaxpr/tij,trj->tri/dot_general | solution.py:115
  430.0 11.6 %fusion.50 = f32[128,8,128]{2,1,0:T(8,128)} fusion(f32[128,128]{1,0:T(8,128)S(1)} %bitcast.93, f32[128,128]{1,0:T(8,128)} %get-tuple-element.121, f32[128,128]{1,0:T(8,128)S(1)} %bitcast.94, f32[128,128]{1,0:T(8,128)} %get-tuple-element.123, f32[128,128]{1,0:T(8,128)S(1)} %bitcast.92, f32[128,128]{1,0:T(8,128)} %get-tuple-element.125, ...), kind=kOutput, calls=%fused_computation.7.clone.1 | convolution fusion | flops 57016320 | bytes 1704065 | tf_op jit(solution)/shard_map/while/body/eval_jaxpr/tij,trj->tri/dot_general | solution.py:115
  447.9 11.6 %fusion.50 = f32[128,8,128]{2,1,0:T(8,128)} fusion(f32[128,128]{1,0:T(8,128)S(1)} %bitcast.93, f32[128,128]{1,0:T(8,128)} %get-tuple-element.121, f32[128,128]{1,0:T(8,128)S(1)} %bitcast.94, f32[128,128]{1,0:T(8,128)} %get-tuple-element.123, f32[128,128]{1,0:T(8,128)S(1)} %bitcast.92, f32[128,128]{1,0:T(8,128)} %get-tuple-element.125, ...), kind=kOutput, calls=%fused_computation.7.clone.1 | convolution fusion | flops 57016320 | bytes 1704065 | tf_op jit(solution)/shard_map/while/body/eval_jaxpr/tij,trj->tri/dot_general | solution.py:115
  465.9 11.6 %fusion.50 = f32[128,8,128]{2,1,0:T(8,128)} fusion(f32[128,128]{1,0:T(8,128)S(1)} %bitcast.93, f32[128,128]{1,0:T(8,128)} %get-tuple-element.121, f32[128,128]{1,0:T(8,128)S(1)} %bitcast.94, f32[128,128]{1,0:T(8,128)} %get-tuple-element.123, f32[128,128]{1,0:T(8,128)S(1)} %bitcast.92, f32[128,128]{1,0:T(8,128)} %get-tuple-element.125, ...), kind=kOutput, calls=%fused_computation.7.clone.1 | convolution fusion | flops 57016320 | bytes 1704065 | tf_op jit(solution)/shard_map/while/body/eval_jaxpr/tij,trj->tri/dot_general | solution.py:115
  483.8 11.6 %fusion.50 = f32[128,8,128]{2,1,0:T(8,128)} fusion(f32[128,128]{1,0:T(8,128)S(1)} %bitcast.93, f32[128,128]{1,0:T(8,128)} %get-tuple-element.121, f32[128,128]{1,0:T(8,128)S(1)} %bitcast.94, f32[128,128]{1,0:T(8,128)} %get-tuple-element.123, f32[128,128]{1,0:T(8,128)S(1)} %bitcast.92, f32[128,128]{1,0:T(8,128)} %get-tuple-element.125, ...), kind=kOutput, calls=%fused_computation.7.clone.1 | convolution fusion | flops 57016320 | bytes 1704065 | tf_op jit(solution)/shard_map/while/body/eval_jaxpr/tij,trj->tri/dot_general | solution.py:115
  501.7 11.6 %fusion.50 = f32[128,8,128]{2,1,0:T(8,128)} fusion(f32[128,128]{1,0:T(8,128)S(1)} %bitcast.93, f32[128,128]{1,0:T(8,128)} %get-tuple-element.121, f32[128,128]{1,0:T(8,128)S(1)} %bitcast.94, f32[128,128]{1,0:T(8,128)} %get-tuple-element.123, f32[128,128]{1,0:T(8,128)S(1)} %bitcast.92, f32[128,128]{1,0:T(8,128)} %get-tuple-element.125, ...), kind=kOutput, calls=%fused_computation.7.clone.1 | convolution fusion | flops 57016320 | bytes 1704065 | tf_op jit(solution)/shard_map/while/body/eval_jaxpr/tij,trj->tri/dot_general | solution.py:115
  519.6 11.6 %fusion.50 = f32[128,8,128]{2,1,0:T(8,128)} fusion(f32[128,128]{1,0:T(8,128)S(1)} %bitcast.93, f32[128,128]{1,0:T(8,128)} %get-tuple-element.121, f32[128,128]{1,0:T(8,128)S(1)} %bitcast.94, f32[128,128]{1,0:T(8,128)} %get-tuple-element.123, f32[128,128]{1,0:T(8,128)S(1)} %bitcast.92, f32[128,128]{1,0:T(8,128)} %get-tuple-element.125, ...), kind=kOutput, calls=%fused_computation.7.clone.1 | convolution fusion | flops 57016320 | bytes 1704065 | tf_op jit(solution)/shard_map/while/body/eval_jaxpr/tij,trj->tri/dot_general | solution.py:115
  537.6 11.6 %fusion.50 = f32[128,8,128]{2,1,0:T(8,128)} fusion(f32[128,128]{1,0:T(8,128)S(1)} %bitcast.93, f32[128,128]{1,0:T(8,128)} %get-tuple-element.121, f32[128,128]{1,0:T(8,128)S(1)} %bitcast.94, f32[128,128]{1,0:T(8,128)} %get-tuple-element.123, f32[128,128]{1,0:T(8,128)S(1)} %bitcast.92, f32[128,128]{1,0:T(8,128)} %get-tuple-element.125, ...), kind=kOutput, calls=%fused_computation.7.clone.1 | convolution fusion | flops 57016320 | bytes 1704065 | tf_op jit(solution)/shard_map/while/body/eval_jaxpr/tij,trj->tri/dot_general | solution.py:115
  555.5 11.6 %fusion.50 = f32[128,8,128]{2,1,0:T(8,128)} fusion(f32[128,128]{1,0:T(8,128)S(1)} %bitcast.93, f32[128,128]{1,0:T(8,128)} %get-tuple-element.121, f32[128,128]{1,0:T(8,128)S(1)} %bitcast.94, f32[128,128]{1,0:T(8,128)} %get-tuple-element.123, f32[128,128]{1,0:T(8,128)S(1)} %bitcast.92, f32[128,128]{1,0:T(8,128)} %get-tuple-element.125, ...), kind=kOutput, calls=%fused_computation.7.clone.1 | convolution fusion | flops 57016320 | bytes 1704065 | tf_op jit(solution)/shard_map/while/body/eval_jaxpr/tij,trj->tri/dot_general | solution.py:115
  573.4 11.6 %fusion.50 = f32[128,8,128]{2,1,0:T(8,128)} fusion(f32[128,128]{1,0:T(8,128)S(1)} %bitcast.93, f32[128,128]{1,0:T(8,128)} %get-tuple-element.121, f32[128,128]{1,0:T(8,128)S(1)} %bitcast.94, f32[128,128]{1,0:T(8,128)} %get-tuple-element.123, f32[128,128]{1,0:T(8,128)S(1)} %bitcast.92, f32[128,128]{1,0:T(8,128)} %get-tuple-element.125, ...), kind=kOutput, calls=%fused_computation.7.clone.1 | convolution fusion | flops 57016320 | bytes 1704065 | tf_op jit(solution)/shard_map/while/body/eval_jaxpr/tij,trj->tri/dot_general | solution.py:115
  591.3 11.6 %fusion.50 = f32[128,8,128]{2,1,0:T(8,128)} fusion(f32[128,128]{1,0:T(8,128)S(1)} %bitcast.93, f32[128,128]{1,0:T(8,128)} %get-tuple-element.121, f32[128,128]{1,0:T(8,128)S(1)} %bitcast.94, f32[128,128]{1,0:T(8,128)} %get-tuple-element.123, f32[128,128]{1,0:T(8,128)S(1)} %bitcast.92, f32[128,128]{1,0:T(8,128)} %get-tuple-element.125, ...), kind=kOutput, calls=%fused_computation.7.clone.1 | convolution fusion | flops 57016320 | bytes 1704065 | tf_op jit(solution)/shard_map/while/body/eval_jaxpr/tij,trj->tri/dot_general | solution.py:115
  609.2 11.6 %fusion.50 = f32[128,8,128]{2,1,0:T(8,128)} fusion(f32[128,128]{1,0:T(8,128)S(1)} %bitcast.93, f32[128,128]{1,0:T(8,128)} %get-tuple-element.121, f32[128,128]{1,0:T(8,128)S(1)} %bitcast.94, f32[128,128]{1,0:T(8,128)} %get-tuple-element.123, f32[128,128]{1,0:T(8,128)S(1)} %bitcast.92, f32[128,128]{1,0:T(8,128)} %get-tuple-element.125, ...), kind=kOutput, calls=%fused_computation.7.clone.1 | convolution fusion | flops 57016320 | bytes 1704065 | tf_op jit(solution)/shard_map/while/body/eval_jaxpr/tij,trj->tri/dot_general | solution.py:115
  627.1 11.6 %fusion.50 = f32[128,8,128]{2,1,0:T(8,128)} fusion(f32[128,128]{1,0:T(8,128)S(1)} %bitcast.93, f32[128,128]{1,0:T(8,128)} %get-tuple-element.121, f32[128,128]{1,0:T(8,128)S(1)} %bitcast.94, f32[128,128]{1,0:T(8,128)} %get-tuple-element.123, f32[128,128]{1,0:T(8,128)S(1)} %bitcast.92, f32[128,128]{1,0:T(8,128)} %get-tuple-element.125, ...), kind=kOutput, calls=%fused_computation.7.clone.1 | convolution fusion | flops 57016320 | bytes 1704065 | tf_op jit(solution)/shard_map/while/body/eval_jaxpr/tij,trj->tri/dot_general | solution.py:115
  645.1 11.6 %fusion.50 = f32[128,8,128]{2,1,0:T(8,128)} fusion(f32[128,128]{1,0:T(8,128)S(1)} %bitcast.93, f32[128,128]{1,0:T(8,128)} %get-tuple-element.121, f32[128,128]{1,0:T(8,128)S(1)} %bitcast.94, f32[128,128]{1,0:T(8,128)} %get-tuple-element.123, f32[128,128]{1,0:T(8,128)S(1)} %bitcast.92, f32[128,128]{1,0:T(8,128)} %get-tuple-element.125, ...), kind=kOutput, calls=%fused_computation.7.clone.1 | convolution fusion | flops 57016320 | bytes 1704065 | tf_op jit(solution)/shard_map/while/body/eval_jaxpr/tij,trj->tri/dot_general | solution.py:115
  (250 shorter events, 229.0 us)
Async XLA Ops:
  6.5 34.5 %copy-start = (bf16[128,64,128]{2,1,0:T(8,128)(2,1)S(1)}, bf16[128,64,128]{2,1,0:T(8,128)(2,1)}, u32[]{:S(2)}) copy-start(bf16[128,64,128]{2,1,0:T(8,128)(2,1)} %param.19) | copy-start | bytes 6291460
  6.5 12.7 %copy-start.5 = (s32[16,16]{1,0:T(8,128)S(1)}, s32[16,16]{1,0:T(8,128)}, u32[]{:S(2)}) copy-start(s32[16,16]{1,0:T(8,128)} %param.21) | copy-start | bytes 3076
  6.5 11.6 %copy-start.7 = (s32[1,8]{1,0:T(1,128)S(1)}, s32[1,8]{1,0:T(1,128)}, u32[]{:S(2)}) copy-start(s32[1,8]{1,0:T(1,128)} %param.24) | copy-start | bytes 100
  6.5 11.6 %copy-start.6 = (s32[512]{0:T(512)S(1)}, s32[512]{0:T(512)}, u32[]{:S(2)}) copy-start(s32[512]{0:T(512)} %param.16) | copy-start | bytes 6148
  6.5 20.3 %all-gather.3.cloned.1.call-start = ((), (), s32[]{:S(2)}) async-start(), calls=%async_computation | async-start | bytes 1310720 | tf_op jit(solution)/shard_map/all_gather | solution.py:66
  31.6 10.6 %copy-start.1 = (bf16[128,64,64]{2,1,0:T(8,128)(2,1)S(1)}, bf16[128,64,64]{2,1,0:T(8,128)(2,1)}, u32[]{:S(2)}) copy-start(bf16[128,64,64]{2,1,0:T(8,128)(2,1)} %copy.23) | copy-start | bytes 3145732
  33.6 20.6 %copy-start.4 = (bf16[64,64,64]{2,1,0:T(8,128)(2,1)S(1)}, bf16[64,64,64]{2,1,0:T(8,128)(2,1)}, u32[]{:S(2)}) copy-start(bf16[64,64,64]{2,1,0:T(8,128)(2,1)} %param.23) | copy-start | bytes 1572868
  35.2 107.1 %collective-permute-start = (bf16[512,11,128]{2,0,1:T(8,128)(2,1)}, bf16[512,11,128]{2,0,1:T(8,128)(2,1)}, u32[]{:S(2)}, u32[]{:S(2)}) collective-permute-start(bf16[512,11,128]{2,0,1:T(8,128)(2,1)} %copy.19), channel_id=1, source_target_pairs={{0,4},{4,8},{8,12},{12,16},{16,20},{20,24},{24,28},{1,5},{5,9},{9,... | collective-permute-start | bytes 4325384 | tf_op jit(solution)/shard_map/ppermute | solution.py:18
  38.5 106.1 %collective-permute-start.1 = (bf16[512,11,128]{2,0,1:T(8,128)(2,1)}, bf16[512,11,128]{2,0,1:T(8,128)(2,1)}, u32[]{:S(2)}, u32[]{:S(2)}) collective-permute-start(bf16[512,11,128]{2,0,1:T(8,128)(2,1)} %copy.19), channel_id=1, source_target_pairs={{4,0},{8,4},{12,8},{16,12},{20,16},{24,20},{28,24},{5,1},{9,5},{13... | collective-permute-start | bytes 4325384 | tf_op jit(solution)/shard_map/ppermute | solution.py:20
  48.1 79.4 %collective-permute-start.2 = (bf16[64,8,64]{2,1,0:T(8,128)(2,1)S(1)}, bf16[64,8,64]{2,1,0:T(8,128)(2,1)}, u32[]{:S(2)}, u32[]{:S(2)}) collective-permute-start(bf16[64,8,64]{2,1,0:T(8,128)(2,1)S(1)} %all_gather.10), channel_id=1, source_target_pairs={{0,4},{4,8},{8,12},{12,16},{16,20},{20,24},{24,28},{1,5},{5,9},{9,... | collective-permute-start | bytes 196616 | tf_op jit(solution)/shard_map/ppermute | solution.py:18
  52.4 75.2 %collective-permute-start.3 = (bf16[64,8,64]{2,1,0:T(8,128)(2,1)S(1)}, bf16[64,8,64]{2,1,0:T(8,128)(2,1)}, u32[]{:S(2)}, u32[]{:S(2)}) collective-permute-start(bf16[64,8,64]{2,1,0:T(8,128)(2,1)S(1)} %all_gather.10), channel_id=1, source_target_pairs={{4,0},{8,4},{12,8},{16,12},{20,16},{24,20},{28,24},{5,1},{9,5},{13... | collective-permute-start | bytes 196616 | tf_op jit(solution)/shard_map/ppermute | solution.py:20
  142.2 4.8 copy-start.2
  172.8 483.8 %copy-start.3 = (f32[128,8,128]{2,1,0:T(8,128)S(1)}, f32[128,8,128]{2,1,0:T(8,128)}, u32[]{:S(2)}) copy-start(f32[128,8,128]{2,1,0:T(8,128)} %fusion.34) | copy-start | bytes 1572868
Sparse Core Ops, SparseCore 0:
  8.9 17.8 all-gather.2
where the time goes:
time: 676 us; the launch traced here: 665 us
  matrix products  325 us (48%)
  local copies, waits for them, and re-layouts  139 us (21%)
  other arithmetic  90 us (13%)
  blocking collectives  76.6 us (11%)
  between operations  13.6 us (2%)
  starting transfers between devices  12.1 us (2%)
  waiting for transfers between devices  8.25 us (1%)
    dot_general x27, matrix products, slot_step(): jnp.einsum('tij,trj->tri', tile, source, preferred_element_type=jnp.float32)  312 us
    gather x27, local copies, waits for them, and re-layouts, slot_step(): rows = nearby[index]  94.2 us
    all_gather x1, blocking collectives, on_device(): all_top = lax.all_gather(top_moment[None], 'leaf', axis=0, tiled=True)  71.2 us
    ge x27, other arithmetic, slot_step(): valid = column >= 0  34.6 us
    concatenate x2, other arithmetic, with_halo(): jnp.concatenate([lax.ppermute(tail, axis, [(i, (i + 1) % count) for i in...  27.5 us
    select_n x27, other arithmetic, slot_step(): rows = nearby[index]  19 us
    sub x27, local copies, waits for them, and re-layouts, kernel_tile(): offset = targets[:, component, :, None] - sources[:, component, None, :]  18.5 us
  transfers between devices with their start and end apart: 5, of which 1 were waited for; matrix products, arithmetic and copies ran while one was open for 5% of the time, Pallas kernels for 0%

commit v1 on v0

v1 whole, which is shorter than its diff:
```python
import functools

import jax
import jax.numpy as jnp
from jax import lax
from jax.experimental import pallas as pl
from jax.experimental.pallas import tpu as pltpu
from jax.sharding import PartitionSpec as P

kernel_scale = 0.07957747154594767
delta_squared = 0.0025
SLOTS = 4
ITEMS = 4
FEATURES = 16


def shift(cells, axis, step):
    count = lax.axis_size(axis)
    if step > 0:
        pairs = [(i, i + 1) for i in range(count - 1)]
    else:
        pairs = [(i + 1, i) for i in range(count - 1)]
    return lax.ppermute(cells, axis, pairs)


def pieces(value):
    high = lax.reduce_precision(value, 8, 7)
    rest = value - high
    middle = lax.reduce_precision(rest, 8, 7)
    return high, middle, rest - middle


def features(planes, target):
    x, y, z = (planes[i].astype(jnp.float32) for i in range(3))
    norm = x * x + y * y + z * z
    one = jnp.ones_like(x)
    if target:
        rows = [x, y, z, *pieces(norm + delta_squared), one, one, one]
    else:
        rows = [-2.0 * x, -2.0 * y, -2.0 * z, one, one, one, *pieces(norm)]
    place = lax.broadcasted_iota(jnp.int32, (1, FEATURES, 1), 1)
    total = jnp.zeros((x.shape[0], FEATURES, x.shape[1]), jnp.float32)
    for k, row in enumerate(rows):
        total = jnp.where(place == k, row[:, None, :], total)
    return total.astype(jnp.bfloat16)


def far_field(moments, lists, couplings, offset):
    valid = lists >= 0
    local = jnp.clip(lists - offset, 0, moments.shape[0] - 1)
    source = jnp.where(valid[..., None, None], moments[local], jnp.zeros((), moments.dtype))
    return jnp.einsum("bkrc,bkcp->brp", source, couplings, preferred_element_type=jnp.float32)


def near_kernel(
    sizes,
    item_leaf,
    item_start,
    steps,
    near,
    inverse,
    counts,
    target_ref,
    own_features,
    halo_features,
    own_charges,
    halo_charges,
    far_ref,
    out_ref,
    feature_table,
    charge_table,
    target_table,
    squared,
    sems,
):
    leaf_dev, group_size, subs = sizes
    copies = [
        pltpu.make_async_copy(
            own_features, feature_table.at[pl.ds(group_size, group_size)], sems.at[0]
        ),
        pltpu.make_async_copy(
            halo_features.at[0], feature_table.at[pl.ds(0, group_size)], sems.at[1]
        ),
        pltpu.make_async_copy(
            halo_features.at[1], feature_table.at[pl.ds(2 * group_size, group_size)], sems.at[2]
        ),
        pltpu.make_async_copy(
            own_charges, charge_table.at[pl.ds(group_size, group_size)], sems.at[3]
        ),
    ]
    for lane in range(subs):
        for side in range(2):
            copies.append(
                pltpu.make_async_copy(
                    halo_charges.at[lane, side, pl.ds(0, leaf_dev)],
                    charge_table.at[pl.ds(2 * side * group_size + lane * leaf_dev, leaf_dev)],
                    sems.at[4 + 2 * lane + side],
                )
            )
    for copy in copies:
        copy.start()

    @pl.loop(0, leaf_dev // 8)
    def _(block):
        for u in range(8):
            t = block * 8 + u
            turned = target_ref[t].astype(jnp.float32).T
            target_table[t] = turned.astype(jnp.bfloat16)

    out_ref[...] = jnp.zeros_like(out_ref)
    for copy in copies:
        copy.wait()
    dead = 3 * group_size
    feature_table[dead] = feature_table[group_size]
    charge_table[dead] = jnp.zeros(charge_table.shape[1:], charge_table.dtype)

    def distances(step):
        for u in range(ITEMS):
            item = step * ITEMS + u
            t = jnp.minimum(item_leaf[item], leaf_dev - 1)
            p = item_start[item]
            rows = [feature_table[near[p + k]] for k in range(SLOTS)]
            squared[u] = jnp.dot(
                target_table[t],
                jnp.concatenate(rows, axis=1),
                preferred_element_type=jnp.float32,
            ).astype(jnp.bfloat16)

    def products(step):
        for u in range(ITEMS):
            item = step * ITEMS + u
            t = jnp.minimum(item_leaf[item], leaf_dev - 1)
            p = item_start[item]
            rows = [charge_table[inverse[near[p + k]]] for k in range(SLOTS)]
            out_ref[t] += lax.dot_general(
                jnp.concatenate(rows, axis=1),
                lax.rsqrt(squared[u]),
                (((1,), (1,)), ((), ())),
                preferred_element_type=jnp.float32,
            )

    distances(0)

    @pl.loop(1, steps[0] + 1)
    def _(step):
        products(step - 1)
        distances(step)

    place = lax.broadcasted_iota(jnp.int32, out_ref.shape[1:], 1)

    @pl.loop(0, leaf_dev // 8)
    def _(block):
        for u in range(8):
            t = block * 8 + u
            total = out_ref[t] * kernel_scale + far_ref[t]
            out_ref[t] = jnp.where(place < counts[t], total, 0.0)


def near_field(targets, own, halo, own_charges, halo_charges, near, inverse, counts, far, subs):
    leaf_dev, slots = near.shape
    group_size = own.shape[0]
    points = own.shape[2]
    dead = 3 * group_size
    chunks = -(-slots // SLOTS)
    live = jnp.sum((near >= 0).astype(jnp.int32), axis=1)
    used = (live + SLOTS - 1) // SLOTS
    ends = jnp.cumsum(used)
    capacity = leaf_dev * chunks + 2 * ITEMS
    item = jnp.arange(capacity, dtype=jnp.int32)
    before = ends[None, :] <= item[:, None]
    leaf = jnp.sum(before.astype(jnp.int32), axis=1)
    first = jnp.max(jnp.where(before, ends[None, :], 0), axis=1)
    row = chunks * SLOTS
    start = jnp.where(leaf < leaf_dev, leaf * row + SLOTS * (item - first), leaf_dev * row)
    steps = ((ends[-1:] + ITEMS - 1) // ITEMS).astype(jnp.int32)
    padded = jnp.pad(
        jnp.where(near >= 0, near, dead), ((0, 1), (0, row - slots)), constant_values=dead
    ).reshape(-1)
    smem = pl.BlockSpec(memory_space=pltpu.SMEM)
    vmem = pl.BlockSpec(memory_space=pltpu.VMEM)
    hbm = pl.BlockSpec(memory_space=pl.ANY)
    rhs = own_charges.shape[1]
    return pl.pallas_call(
        functools.partial(near_kernel, (leaf_dev, group_size, subs)),
        out_shape=jax.ShapeDtypeStruct((leaf_dev, rhs, points), jnp.float32),
        in_specs=[smem] * 6 + [vmem, hbm, hbm, hbm, hbm, vmem],
        out_specs=vmem,
        scratch_shapes=[
            pltpu.VMEM((dead + 1, FEATURES, points), jnp.bfloat16),
            pltpu.VMEM((dead + 1, rhs, points), jnp.bfloat16),
            pltpu.VMEM((leaf_dev, points, FEATURES), jnp.bfloat16),
            pltpu.VMEM((ITEMS, points, SLOTS * points), jnp.bfloat16),
            pltpu.SemaphoreType.DMA((4 + 2 * subs,)),
        ],
        compiler_params=pltpu.CompilerParams(vmem_limit_bytes=48 * 1024 * 1024),
        name="near_field",
    )(
        leaf.astype(jnp.int32),
        start.astype(jnp.int32),
        steps,
        padded,
        inverse,
        counts,
        targets,
        own,
        halo,
        own_charges,
        halo_charges,
        far,
    )


def on_device(
    coords,
    charges,
    counts,
    morton,
    near_list,
    basis,
    transfer1,
    far2_list,
    coupling2,
    transfer2,
    far3_list,
    coupling3,
):
    lane = lax.axis_index("sub")
    group = lax.axis_index("leaf")
    subs = lax.axis_size("sub")
    leaf_dev, rhs_count, points = charges.shape
    rank_size = basis.shape[1]
    group_size = coords.shape[0]
    clusters = far2_list.shape[0]
    group_boxes = transfer2.shape[0]
    start = lane * leaf_dev

    slot = lax.dynamic_slice_in_dim(morton, start, leaf_dev, 0)
    arriving_counts = counts[slot]
    place = jnp.arange(points, dtype=jnp.int32)
    masked = jnp.where(
        place[None, None, :] < arriving_counts[:, None, None], charges, jnp.zeros((), charges.dtype)
    )
    arrived = lax.all_gather(masked, "sub", axis=0, tiled=True)
    planes = coords.transpose(1, 0, 2)
    own_planes = lax.dynamic_slice_in_dim(planes, start, leaf_dev, 1)
    bundle = jnp.concatenate([masked, own_planes.reshape(-1, rhs_count, points)], axis=0)
    sides = jnp.stack([shift(bundle, "leaf", 1), shift(bundle, "leaf", -1)])
    halo = lax.all_gather(sides, "sub", axis=0)

    inverse = (
        jnp.zeros((group_size,), jnp.int32).at[morton].set(jnp.arange(group_size, dtype=jnp.int32))
    )
    all_inverse = jnp.concatenate(
        [
            shift(inverse, "leaf", 1),
            inverse + group_size,
            shift(inverse, "leaf", -1) + 2 * group_size,
            jnp.full((1,), 3 * group_size, jnp.int32),
        ]
    )
    own_features = features(planes, False)
    targets = features(own_planes, True)
    halo_planes = halo[:, :, leaf_dev:].reshape(subs, 2, 3, leaf_dev, points)
    halo_planes = halo_planes.transpose(2, 1, 0, 3, 4).reshape(3, 2 * group_size, points)
    halo_features = features(halo_planes, False).reshape(2, group_size, FEATURES, points)

    own_charges = arrived[lax.dynamic_slice_in_dim(inverse, start, leaf_dev, 0)]
    transfer_boxed = transfer1.reshape(clusters, 8, rank_size, rank_size)
    leaf_moments = jnp.einsum(
        "trp,tkp->trk", own_charges, basis, preferred_element_type=jnp.float32
    ).astype(jnp.bfloat16)
    box_moments = jnp.einsum(
        "bnrc,bncp->brp",
        leaf_moments.reshape(clusters, 8, rhs_count, rank_size),
        transfer_boxed,
        preferred_element_type=jnp.float32,
    ).astype(jnp.bfloat16)
    group_moments = lax.all_gather(box_moments, "sub", axis=0, tiled=True)
    top_moment = jnp.einsum(
        "brc,bcp->rp", group_moments, transfer2, preferred_element_type=jnp.float32
    ).astype(jnp.bfloat16)
    all_top = lax.all_gather(top_moment[None], "leaf", axis=0, tiled=True)
    near_boxes = jnp.concatenate(
        [shift(group_moments, "leaf", 1), group_moments, shift(group_moments, "leaf", -1)], axis=0
    )
    top_field = far_field(all_top, far3_list, coupling3, 0).astype(jnp.bfloat16)
    box_far = far_field(near_boxes, far2_list, coupling2, (group - 1) * group_boxes)
    own_transfer = lax.dynamic_slice_in_dim(transfer2, lane * clusters, clusters, 0)
    box_local = (
        box_far
        + jnp.einsum("rp,bcp->brc", top_field[0], own_transfer, preferred_element_type=jnp.float32)
    ).astype(jnp.bfloat16)
    leaf_local = jnp.einsum(
        "brp,bncp->bnrc", box_local, transfer_boxed, preferred_element_type=jnp.float32
    ).astype(jnp.bfloat16)
    leaf_local = leaf_local.reshape(leaf_dev, rhs_count, rank_size)
    far_part = jnp.einsum("trk,tkp->trp", leaf_local, basis, preferred_element_type=jnp.float32)

    base = (group - 1) * group_size
    near = jnp.where(near_list >= 0, near_list - base, -1)
    own_counts = lax.dynamic_slice_in_dim(counts, start, leaf_dev, 0)
    return near_field(
        targets,
        own_features,
        halo_features,
        arrived,
        halo,
        near,
        all_inverse,
        own_counts,
        far_part,
        subs,
    )


def solution(mesh):
    return jax.shard_map(
        on_device,
        mesh=mesh,
        in_specs=(
            P("leaf", None, None),
            P(("leaf", "sub"), None, None),
            P("leaf"),
            P("leaf"),
            P(("leaf", "sub"), None),
            P(("leaf", "sub"), None, None),
            P(("leaf", "sub"), None, None),
            P(("leaf", "sub"), None),
            P(("leaf", "sub"), None, None, None),
            P("leaf", None, None),
            P("leaf", None),
            P("leaf", None, None, None),
        ),
        out_specs=P(("leaf", "sub"), None, None),
        check_vma=False,
    )
```

time: 676 us -> 196 us (0.29)
  the two profiles are of different devices: /device:TPU:10 before, /device:TPU:4 now
where the time goes in v1:
time: 196 us; the launch traced here: 194 us
  Pallas kernels  78.9 us (40%)
  blocking collectives  35.5 us (18%)
  starting transfers between devices  17.7 us (9%)
  local copies, waits for them, and re-layouts  17.3 us (9%)
  other arithmetic  17.1 us (9%)
  between operations  14.4 us (7%)
  matrix products  10 us (5%)
  waiting for transfers between devices  3.23 us (2%)
    pallas_call x1, Pallas kernels, near_field(): pl.pallas_call(functools.partial(near_kernel, (leaf_dev, group_size, subs...  78.9 us
    all_gather x1, blocking collectives, on_device(): all_top = lax.all_gather(top_moment[None], 'leaf', axis=0, tiled=True)  29.4 us
    ppermute x6, starting transfers between devices, shift(): return lax.ppermute(cells, axis, pairs)  17.7 us
    convert_element_type x3, other arithmetic, features(): return total.astype(jnp.bfloat16)  11.3 us
    all_gather x1, blocking collectives, on_device(): group_moments = lax.all_gather(box_moments, 'sub', axis=0, tiled=True)  6.1 us
    unnamed x26, local copies, waits for them, and re-layouts  5.35 us
  transfers between devices with their start and end apart: 8, of which 1 were waited for; matrix products, arithmetic and copies ran while one was open for 16% of the time, Pallas kernels for 0%

profile of v1, /device:TPU:4, one launch (start us, length us, event | category | flops | bytes accessed | tf_op | source)
XLA Modules:
  0.0 194.2 jit_solution(6436309867674391469)
XLA Ops:
  6.6 0.9 compare_select_fusion.5
  7.5 1.6 gather_fusion
  9.3 0.9 constant_dynamic-slice_fusion
  10.2 1.0 broadcast_select_fusion
  11.3 4.2 %collective-permute-start.2 = (bf16[176,8,128]{2,1,0:T(8,128)(2,1)S(1)}, bf16[176,8,128]{2,1,0:T(8,128)(2,1)}, u32[]{:S(2)}, u32[]{:S(2)}) collective-permute-start(bf16[176,8,128]{2,1,0:T(8,128)(2,1)S(1)} %pad_maximum_fusion.2), channel_id=1, source_target_pairs={{0,4},{4,8},{8,12},{12,16},{16,20},{20,24},{24,28},{1,5},{5,9},{9,... | collective-permute-start | bytes 1081352 | tf_op jit(solution)/shard_map/ppermute | solution.py:23
  15.4 1.3 collective-permute-start.3
  16.8 2.4 %scatter_custom_fusion = s32[512]{0:T(512)S(1)} fusion(s32[512]{0:T(512)S(1)} %compare_select_fusion.2, s32[512]{0:T(512)S(1)} %iota.88, s32[]{:T(128)} %constant.36.clone.1), kind=kCustom, calls=%fused_computation.96 | custom fusion | bytes 2052 | tf_op jit(solution)/shard_map/scatter | solution.py:251
  19.3 1.3 collective-permute-start.1
  20.6 5.2 %collective-permute-start = (s32[512]{0:T(512)S(1)}, s32[512]{0:T(512)S(1)}, u32[]{:S(2)}, u32[]{:S(2)}) collective-permute-start(s32[512]{0:T(512)S(1)} %scatter_custom_fusion), channel_id=1, source_target_pairs={{0,4},{4,8},{8,12},{12,16},{16,20},{20,24},{24,28},{1,5},{5,9},{9,... | collective-permute-start | bytes 6152 | tf_op jit(solution)/shard_map/ppermute | solution.py:23
  26.9 3.2 %collective-permute-done.2 = bf16[176,8,128]{2,1,0:T(8,128)(2,1)} collective-permute-done((bf16[176,8,128]{2,1,0:T(8,128)(2,1)S(1)}, bf16[176,8,128]{2,1,0:T(8,128)(2,1)}, u32[]{:S(2)}, u32[]{:S(2)}) %collective-permute-start.2) | collective-permute-done | bytes 360480 | tf_op jit(solution)/shard_map/ppermute | solution.py:23
  30.1 2.0 %pad_maximum_fusion = bf16[2,176,8,128]{3,2,1,0:T(8,128)(2,1)} fusion(bf16[1,176,8,128]{3,2,1,0:T(8,128)(2,1)} %bitcast.16, bf16[1,176,8,128]{3,2,1,0:T(8,128)(2,1)} %bitcast.15), kind=kLoop, calls=%fused_computation.23 | loop fusion | flops 360448 | bytes 1441792 | tf_op jit(solution)/shard_map/stack | solution.py:247
  32.5 0.9 select_convert_fusion.2.target_ref
  33.4 3.9 %select_convert_fusion.1.own_features = bf16[512,16,128]{2,1,0:T(8,128)(2,1)} fusion(bf16[512,128]{1,0:T(8,128)(2,1)S(1)} %get-tuple-element.17, bf16[512,128]{1,0:T(8,128)(2,1)S(1)} %get-tuple-element.16, bf16[512,128]{1,0:T(8,128)(2,1)S(1)} %get-tuple-element.15, f32[512,128]{1,0:T(8,128)S(1)} %get-tuple-element.8, bf16[512,128]{1,0:T(8,128)(2,1)S(1)} %fusion.38, ...), kind=kLoop, calls=%fused_computation.6 | loop fusion | flops 9437184 | bytes 3014800 | tf_op jit(solution)/shard_map/convert_element_type | solution.py:45
  37.4 0.5 slice.56
  38.4 0.8 dynamic_slice.15.counts
  39.2 4.7 %copy.27 = bf16[128,64,64]{2,1,0:T(8,128)(2,1)} copy(bf16[128,64,64]{0,2,1:T(8,128)(2,1)} %param.18) | data formatting | bytes 2097152 | tf_op args[6]
  44.2 2.0 %gather_fusion.1 = bf16[128,8,128]{2,1,0:T(8,128)(2,1)S(1)} fusion(bf16[512,8,128]{2,1,0:T(8,128)(2,1)} %all-gather.5.cloned.1.call-done.own_charges, s32[1024]{0:T(1024)S(1)} %pad_clamp_fusion.2), kind=kCustom, calls=%fused_computation.1 | custom fusion | bytes 524800 | tf_op jit(solution)/shard_map/gather | solution.py:267
  46.3 1.2 convolution_convert_fusion.1
  47.4 0.5 copy-done.3
  47.9 0.4 fusion.2
  48.3 6.1 %all_gather.18 = bf16[64,8,64]{2,1,0:T(8,128)(2,1)S(1)} all-gather(bf16[16,8,64]{2,1,0:T(8,128)(2,1)S(1)} %fusion.2), channel_id=1, replica_groups=mesh['leaf'=8,'sub'=4] {'sub'}, dimensions={0}, use_global_device_ids=true | all-gather | bytes 81920 | tf_op jit(solution)/shard_map/all_gather | solution.py:278
  54.4 4.5 %collective-permute-start.4 = (bf16[64,8,64]{2,1,0:T(8,128)(2,1)S(1)}, bf16[64,8,64]{2,1,0:T(8,128)(2,1)S(1)}, u32[]{:S(2)}, u32[]{:S(2)}) collective-permute-start(bf16[64,8,64]{2,1,0:T(8,128)(2,1)S(1)} %all_gather.18), channel_id=1, source_target_pairs={{0,4},{4,8},{8,12},{12,16},{16,20},{20,24},{24,28},{1,5},{5,9},{9,... | collective-permute-start | bytes 196616 | tf_op jit(solution)/shard_map/ppermute | solution.py:23
  58.9 1.3 collective-permute-start.5
  60.5 29.4 %all-gather.1 = bf16[64,64]{1,0:T(8,128)(2,1)S(1)} all-gather(bf16[8,64]{1,0:T(8,128)(2,1)S(1)} %fusion.4), channel_id=3, replica_groups=mesh['leaf'=8,'sub'=4] {'leaf'}, dimensions={0}, use_global_device_ids=true | all-gather | bytes 9216 | tf_op jit(solution)/shard_map/all_gather | solution.py:282
  89.9 0.6 gather_fusion.3
  90.8 1.6 gather_fusion.2
  92.4 3.5 %convolution_bitcast_fusion.1 = f32[16,8,64]{2,1,0:T(8,128)S(1)} fusion(bf16[16,16,64,64]{3,2,1,0:T(8,128)(2,1)} %param.20, bf16[16,16,8,64]{3,2,1,0:T(8,128)(2,1)} %bitcast.159, pred[16,16]{1,0:T(8,128)(4,1)S(1)} %broadcast_compare_fusion), kind=kOutput, calls=%fused_computation.11 | convolution fusion | flops 16908288 | bytes 2392320 | tf_op jit(solution)/shard_map/bkrc,bkcp->brp/dot_general | solution.py:52
  95.9 3.6 %convolution_convert_fusion = bf16[16,8,8,64]{3,1,2,0:T(8,128)(2,1)S(1)} fusion(bf16[16,8,64,64]{3,2,1,0:T(8,128)(2,1)} %bitcast.145, f32[16,8,64]{2,1,0:T(8,128)S(1)} %convolution_bitcast_fusion.1, bf16[8,64,1]{1,0,2:T(8,128)(2,1)S(1)} %fusion.6, bf16[64,64,64]{2,1,0:T(8,128)(2,1)} %param.21, s32[]{:T(128)S(6)} %select_n.204), kind=kOutput, calls=%fused_computation.7 | convolution fusion | flops 9519104 | bytes 2524164 | tf_op jit(solution)/shard_map/brp,bncp->bnrc/dot_general | solution.py:293
  99.5 0.7 fusion.40.far_ref
  100.2 1.2 slice.63
  102.0 6.4 %select_convert_fusion.halo_features = bf16[2,512,16,128]{3,2,1,0:T(8,128)(2,1)} fusion(bf16[2,512,128]{2,1,0:T(8,128)(2,1)S(1)} %bitcast.158, bf16[2,512,128]{2,1,0:T(8,128)(2,1)S(1)} %bitcast.157, bf16[2,512,128]{2,1,0:T(8,128)(2,1)S(1)} %bitcast.156, bf16[2,512,128]{2,1,0:T(8,128)(2,1)S(1)} %get-tuple-element.14, ...), kind=kLoop, calls=%fused_computation.5 | loop fusion | flops 18874368 | bytes 5767312 | tf_op jit(solution)/shard_map/convert_element_type | solution.py:45
  108.5 78.9 %near_field.1 = f32[128,8,128]{2,1,0:T(8,128)} custom-call(s32[904]{0:T(1024)S(1)} %get-tuple-element.6.item_leaf, s32[904]{0:T(1024)S(1)} %add_select_fusion.item_start, s32[1]{0:T(128)S(6)} %select_n.168.steps, s32[3612]{0:T(1024)S(1)} %reshape.380.near, s32[1537]{0:T(1024)S(1)} %pad_add_fusion.inverse, s32[128]{0:T(128)S(1)} %dynamic_slice.15.counts, ...), custom_call_target="tpu_custom_call" | custom-call | tf_op jit(solution)/shard_map/near_field/pallas_call | solution.py:183
  (79 shorter events, 3.2 us)
Async XLA Ops:
  6.5 39.7 %copy-start = (bf16[128,64,128]{2,1,0:T(8,128)(2,1)S(1)}, bf16[128,64,128]{2,1,0:T(8,128)(2,1)}, u32[]{:S(2)}) copy-start(bf16[128,64,128]{2,1,0:T(8,128)(2,1)} %param.17) | copy-start | bytes 6291460
  6.5 10.3 %copy-start.9 = (s32[512]{0:T(512)S(1)}, s32[512]{0:T(512)}, u32[]{:S(2)}) copy-start(s32[512]{0:T(512)} %param.15) | copy-start | bytes 6148
  6.5 20.3 %copy-start.4 = (bf16[512,3,128]{2,0,1:T(8,128)(2,1)S(1)}, bf16[512,3,128]{2,0,1:T(8,128)(2,1)}, u32[]{:S(2)}) copy-start(bf16[512,3,128]{2,0,1:T(8,128)(2,1)} %param.12) | copy-start | bytes 1179652
  6.5 19.3 %copy-start.8 = (s32[128,27]{0,1:T(8,128)S(1)}, s32[128,27]{0,1:T(8,128)}, u32[]{:S(2)}) copy-start(s32[128,27]{0,1:T(8,128)} %param.16) | copy-start | bytes 41476
  6.5 19.6 %copy-start.7 = (s32[16,16]{1,0:T(8,128)S(1)}, s32[16,16]{1,0:T(8,128)}, u32[]{:S(2)}) copy-start(s32[16,16]{1,0:T(8,128)} %param.19) | copy-start | bytes 3076
  6.5 19.8 %copy-start.11 = (s32[1,8]{1,0:T(1,128)S(1)}, s32[1,8]{1,0:T(1,128)}, u32[]{:S(2)}) copy-start(s32[1,8]{1,0:T(1,128)} %param.22) | copy-start | bytes 100
  6.6 37.6 %all-gather.5.cloned.1.call-start = ((), (), s32[]{:S(2)}) async-start(), calls=%async_computation | async-start | bytes 1310720 | tf_op jit(solution)/shard_map/all_gather | solution.py:243
  11.2 5.5 %copy-start.5 = (bf16[128,8,128]{2,1,0:T(8,128)(2,1)}, bf16[128,8,128]{2,1,0:T(8,128)(2,1)S(1)}, u32[]{:S(2)}) copy-start(bf16[128,8,128]{2,1,0:T(8,128)(2,1)S(1)} %broadcast_select_fusion) | copy-start | bytes 786436
  11.3 18.8 %collective-permute-start.2 = (bf16[176,8,128]{2,1,0:T(8,128)(2,1)S(1)}, bf16[176,8,128]{2,1,0:T(8,128)(2,1)}, u32[]{:S(2)}, u32[]{:S(2)}) collective-permute-start(bf16[176,8,128]{2,1,0:T(8,128)(2,1)S(1)} %pad_maximum_fusion.2), channel_id=1, source_target_pairs={{0,4},{4,8},{8,12},{12,16},{16,20},{20,24},{24,28},{1,5},{5,9},{9,... | collective-permute-start | bytes 1081352 | tf_op jit(solution)/shard_map/ppermute | solution.py:23
  15.4 14.7 %collective-permute-start.3 = (bf16[176,8,128]{2,1,0:T(8,128)(2,1)S(1)}, bf16[176,8,128]{2,1,0:T(8,128)(2,1)}, u32[]{:S(2)}, u32[]{:S(2)}) collective-permute-start(bf16[176,8,128]{2,1,0:T(8,128)(2,1)S(1)} %pad_maximum_fusion.2), channel_id=1, source_target_pairs={{4,0},{8,4},{12,8},{16,12},{20,16},{24,20},{28,24},{5,1},{9,5},{13... | collective-permute-start | bytes 1081352 | tf_op jit(solution)/shard_map/ppermute | solution.py:23
  16.7 83.5 %all-gather.7.cloned.1.call-start = ((), (), s32[]{:S(2)}) async-start(), calls=%async_computation.1 | async-start | bytes 3604480 | tf_op jit(solution)/shard_map/all_gather | solution.py:248
  19.3 24.9 %collective-permute-start.1 = (s32[512]{0:T(512)S(1)}, s32[512]{0:T(512)S(1)}, u32[]{:S(2)}, u32[]{:S(2)}) collective-permute-start(s32[512]{0:T(512)S(1)} %scatter_custom_fusion), channel_id=1, source_target_pairs={{4,0},{8,4},{12,8},{16,12},{20,16},{24,20},{28,24},{5,1},{9,5},{13... | collective-permute-start | bytes 6152 | tf_op jit(solution)/shard_map/ppermute | solution.py:23
  20.6 23.6 %collective-permute-start = (s32[512]{0:T(512)S(1)}, s32[512]{0:T(512)S(1)}, u32[]{:S(2)}, u32[]{:S(2)}) collective-permute-start(s32[512]{0:T(512)S(1)} %scatter_custom_fusion), channel_id=1, source_target_pairs={{0,4},{4,8},{8,12},{12,16},{16,20},{20,24},{24,28},{1,5},{5,9},{9,... | collective-permute-start | bytes 6152 | tf_op jit(solution)/shard_map/ppermute | solution.py:23
  46.2 1.7 copy-start.3
  46.2 14.0 %copy-start.6 = (bf16[64,64,64]{2,1,0:T(8,128)(2,1)S(1)}, bf16[64,64,64]{2,1,0:T(8,128)(2,1)}, u32[]{:S(2)}) copy-start(bf16[64,64,64]{2,1,0:T(8,128)(2,1)} %param.21) | copy-start | bytes 1572868
  47.4 43.0 %copy-start.10 = (bf16[1,8,64,64]{3,2,1,0:T(8,128)(2,1)S(1)}, bf16[1,8,64,64]{3,2,1,0:T(8,128)(2,1)}, u32[]{:S(2)}) copy-start(bf16[1,8,64,64]{3,2,1,0:T(8,128)(2,1)} %param.23) | copy-start | bytes 196612
  54.4 36.3 %collective-permute-start.4 = (bf16[64,8,64]{2,1,0:T(8,128)(2,1)S(1)}, bf16[64,8,64]{2,1,0:T(8,128)(2,1)S(1)}, u32[]{:S(2)}, u32[]{:S(2)}) collective-permute-start(bf16[64,8,64]{2,1,0:T(8,128)(2,1)S(1)} %all_gather.18), channel_id=1, source_target_pairs={{0,4},{4,8},{8,12},{12,16},{16,20},{20,24},{24,28},{1,5},{5,9},{9,... | collective-permute-start | bytes 196616 | tf_op jit(solution)/shard_map/ppermute | solution.py:23
  58.9 31.8 %collective-permute-start.5 = (bf16[64,8,64]{2,1,0:T(8,128)(2,1)S(1)}, bf16[64,8,64]{2,1,0:T(8,128)(2,1)S(1)}, u32[]{:S(2)}, u32[]{:S(2)}) collective-permute-start(bf16[64,8,64]{2,1,0:T(8,128)(2,1)S(1)} %all_gather.18), channel_id=1, source_target_pairs={{4,0},{8,4},{12,8},{16,12},{20,16},{24,20},{28,24},{5,1},{9,5},{13... | collective-permute-start | bytes 196616 | tf_op jit(solution)/shard_map/ppermute | solution.py:23
  102.0 6.5 %copy-start.1 = (bf16[512,16,128]{2,1,0:T(8,128)(2,1)S(1)}, bf16[512,16,128]{2,1,0:T(8,128)(2,1)}, u32[]{:S(2)}) copy-start(bf16[512,16,128]{2,1,0:T(8,128)(2,1)} %select_convert_fusion.1.own_features) | copy-start | bytes 6291460
  102.0 6.5 %copy-start.2 = (bf16[512,8,128]{2,1,0:T(8,128)(2,1)S(1)}, bf16[512,8,128]{2,1,0:T(8,128)(2,1)}, u32[]{:S(2)}) copy-start(bf16[512,8,128]{2,1,0:T(8,128)(2,1)} %all-gather.5.cloned.1.call-done.own_charges) | copy-start | bytes 3145732
Sparse Core Ops, SparseCore 0:
  16.9 17.9 all-gather.4
  36.4 27.7 all-gather.6

commit v2 on v1

--- a/solution.py
+++ b/solution.py
@@ -14,13 +14,7 @@
 FEATURES = 16
 
 
-def shift(cells, axis, step):
-    count = lax.axis_size(axis)
-    if step > 0:
-        pairs = [(i, i + 1) for i in range(count - 1)]
-    else:
-        pairs = [(i + 1, i) for i in range(count - 1)]
-    return lax.ppermute(cells, axis, pairs)
+MESH = pl.DeviceIdType.MESH
 
 
 def pieces(value):
@@ -45,11 +39,298 @@
     return total.astype(jnp.bfloat16)
 
 
-def far_field(moments, lists, couplings, offset):
-    valid = lists >= 0
-    local = jnp.clip(lists - offset, 0, moments.shape[0] - 1)
-    source = jnp.where(valid[..., None, None], moments[local], jnp.zeros((), moments.dtype))
-    return jnp.einsum("bkrc,bkcp->brp", source, couplings, preferred_element_type=jnp.float32)
+NT = (((1,), (1,)), ((), ()))
+
+
+def flip(lane, bit):
+    return lane + bit - 2 * bit * ((lane // bit) % 2)
+
+
+def matmul(left, right):
+    return jnp.dot(left, right, preferred_element_type=jnp.float32)
+
+
+def tree_kernel(
+    groups,
+    subs,
+    positions,
+    far2,
+    far3,
+    bundle,
+    inverse,
+    basis,
+    transfer1,
+    coupling2,
+    transfer2,
+    coupling3,
+    own_table,
+    halo,
+    halo_inverse,
+    far_ref,
+    boxes,
+    tops,
+    box_far,
+    local_sems,
+    own_sems,
+    side_sems,
+    inverse_sems,
+    halo_sems,
+    box_sems,
+    top_sems,
+):
+    group = lax.axis_index("leaf")
+    lane = lax.axis_index("sub")
+    leaf_dev = basis.shape[0]
+    clusters = transfer1.shape[0]
+    slots2 = far2.shape[1]
+    slots3 = far3.shape[1]
+    rank = basis.shape[1]
+    before = (group + groups - 1) % groups
+    after = (group + 1) % groups
+    around = [((lane + d) % subs) for d in range(1, subs)]
+
+    barrier = pltpu.get_barrier_semaphore()
+    peers = [(group, other) for other in around]
+    peers += [(side, other) for side in (before, after) for other in around]
+    peers += [((group + d) % groups, lane) for d in range(1, groups)]
+    for peer in peers:
+        pl.semaphore_signal(barrier, inc=1, device_id=peer, device_id_type=MESH)
+    pl.semaphore_wait(barrier, len(peers))
+
+    def send(source, target, sems, index, device):
+        copy = pltpu.make_async_remote_copy(
+            src_ref=source,
+            dst_ref=target,
+            send_sem=sems.at[0, index],
+            recv_sem=sems.at[1, index],
+            device_id=device,
+            device_id_type=MESH,
+        )
+        copy.start()
+        return copy
+
+    started = []
+    bits = []
+    bit = subs // 2
+    while bit:
+        bits.append(bit)
+        bit //= 2
+
+    charges = bundle.at[pl.ds(0, leaf_dev)]
+    keep = [
+        pltpu.make_async_copy(charges, own_table.at[lane], local_sems.at[0]),
+    ]
+    for copy in keep:
+        copy.start()
+    first = send(charges, own_table.at[lane], own_sems, 0, (group, flip(lane, bits[0])))
+    started.append(first)
+    sides = [
+        send(bundle, halo.at[0, lane], side_sems, 0, (after, lane)),
+        send(bundle, halo.at[1, lane], side_sems, 1, (before, lane)),
+        send(inverse, halo_inverse.at[0], inverse_sems, 0, (after, lane)),
+        send(inverse, halo_inverse.at[1], inverse_sems, 1, (before, lane)),
+    ]
+    started += sides
+    for copy in keep:
+        copy.wait()
+    first.wait_recv()
+    held = [lane, flip(lane, bits[0])]
+    count = 1
+    for bit in bits[1:]:
+        copies = []
+        for block in held:
+            copies.append(
+                send(
+                    own_table.at[block],
+                    own_table.at[block],
+                    own_sems,
+                    count,
+                    (group, flip(lane, bit)),
+                )
+            )
+            count += 1
+        started += copies
+        for copy in copies:
+            copy.wait_recv()
+        held = held + [flip(block, bit) for block in held]
+
+    mine = boxes.at[1, lane]
+
+    @pl.loop(0, clusters)
+    def _(b):
+        moments = []
+        for u in range(8):
+            position = positions[b * 8 + u]
+            source = own_table[position // leaf_dev, position % leaf_dev]
+            moments.append(
+                lax.dot_general(
+                    source, basis[b * 8 + u], NT, preferred_element_type=jnp.float32
+                ).astype(jnp.bfloat16)
+            )
+        boxes[1, lane, b] = matmul(jnp.concatenate(moments, axis=1), transfer1[b]).astype(
+            jnp.bfloat16
+        )
+
+    copies = []
+    for other in around:
+        copies.append(send(mine, boxes.at[1, lane], box_sems, len(copies), (group, other)))
+    for other in [lane] + around:
+        copies.append(send(mine, boxes.at[0, lane], box_sems, len(copies), (after, other)))
+        copies.append(send(mine, boxes.at[2, lane], box_sems, len(copies), (before, other)))
+    started += copies
+    box_copies = copies
+
+    for copy in sides:
+        copy.wait_recv()
+    held = [lane]
+    count = 0
+    halo_copies = []
+
+    def forward(bit, held, count):
+        copies = []
+        for block in held:
+            for side in range(2):
+                copies.append(
+                    send(
+                        halo.at[side, block],
+                        halo.at[side, block],
+                        halo_sems,
+                        count,
+                        (group, flip(lane, bit)),
+                    )
+                )
+                count += 1
+        return copies, held + [flip(block, bit) for block in held], count
+
+    halo_copies, held, count = forward(bits[0], held, count)
+    started += halo_copies
+
+    for copy in box_copies:
+        copy.wait_recv()
+
+    def top_step(chunk, total):
+        cells = [boxes[1, chunk * 8 // clusters, chunk * 8 % clusters + u] for u in range(8)]
+        return total + matmul(jnp.concatenate(cells, axis=1), transfer2[chunk])
+
+    top = lax.fori_loop(
+        0, subs * clusters // 8, top_step, jnp.zeros((bundle.shape[1], rank), jnp.float32)
+    )
+    tops[group] = top.astype(jnp.bfloat16)
+    top_copies = [
+        send(tops.at[group], tops.at[group], top_sems, d - 1, ((group + d) % groups, lane))
+        for d in range(1, groups)
+    ]
+    started += top_copies
+
+    @pl.loop(0, clusters)
+    def _(b):
+        cells = []
+        for k in range(slots2):
+            name = far2[b, k]
+            local = jnp.clip(name - (group - 1) * subs * clusters, 0, 3 * subs * clusters - 1)
+            side = local // (subs * clusters)
+            rest = local % (subs * clusters)
+            cell = boxes[side, rest // clusters, rest % clusters]
+            cells.append(jnp.where(name >= 0, cell, jnp.zeros_like(cell)))
+        box_far[b] = matmul(jnp.concatenate(cells, axis=1), coupling2[b])
+
+    for bit in bits[1:]:
+        for copy in halo_copies:
+            copy.wait_recv()
+        halo_copies, held, count = forward(bit, held, count)
+        started += halo_copies
+
+    for copy in top_copies:
+        copy.wait_recv()
+    cells = []
+    for k in range(slots3):
+        name = far3[0, k]
+        cell = tops[jnp.maximum(name, 0)]
+        cells.append(jnp.where(name >= 0, cell, jnp.zeros_like(cell)))
+    top_field = matmul(jnp.concatenate(cells, axis=1), coupling3[...]).astype(jnp.bfloat16)
+
+    @pl.loop(0, clusters)
+    def _(b):
+        at = lane * clusters + b
+        parent = transfer2[at // 8, pl.ds(pl.multiple_of(at % 8 * rank, rank), rank)]
+        local = box_far[b] + lax.dot_general(
+            top_field, parent, NT, preferred_element_type=jnp.float32
+        )
+        leaves = lax.dot_general(
+            local.astype(jnp.bfloat16), transfer1[b], NT, preferred_element_type=jnp.float32
+        ).astype(jnp.bfloat16)
+        for u in range(8):
+            far_ref[b * 8 + u] = matmul(leaves[:, u * rank : (u + 1) * rank], basis[b * 8 + u])
+
+    for copy in halo_copies:
+        copy.wait_recv()
+    for copy in started:
+        copy.wait_send()
+
+
+def tree_passes(
+    groups,
+    subs,
+    positions,
+    far2_list,
+    far3_list,
+    bundle,
+    inverse,
+    basis,
+    transfer1,
+    coupling2,
+    transfer2,
+    coupling3,
+):
+    leaf_dev, rank, points = basis.shape
+    clusters = far2_list.shape[0]
+    rhs = bundle.shape[1]
+    smem = pl.BlockSpec(memory_space=pltpu.SMEM)
+    vmem = pl.BlockSpec(memory_space=pltpu.VMEM)
+    hbm = pl.BlockSpec(memory_space=pl.ANY)
+    dma = pltpu.SemaphoreType.DMA
+    return pl.pallas_call(
+        functools.partial(tree_kernel, groups, subs),
+        out_shape=(
+            jax.ShapeDtypeStruct((subs, leaf_dev, rhs, points), jnp.bfloat16),
+            jax.ShapeDtypeStruct((2, subs) + bundle.shape, jnp.bfloat16),
+            jax.ShapeDtypeStruct((2,) + inverse.shape, jnp.int32),
+            jax.ShapeDtypeStruct((leaf_dev, rhs, points), jnp.float32),
+        ),
+        in_specs=[smem] * 3 + [hbm] * 2 + [vmem] * 5,
+        out_specs=(vmem, hbm, hbm, vmem),
+        scratch_shapes=[
+            pltpu.VMEM((3, subs, clusters, rhs, rank), jnp.bfloat16),
+            pltpu.VMEM((groups, rhs, rank), jnp.bfloat16),
+            pltpu.VMEM((clusters, rhs, rank), jnp.float32),
+            dma((1,)),
+            dma((2, subs - 1)),
+            dma((2, 2)),
+            dma((2, 2)),
+            dma((2, 2 * (subs - 1))),
+            dma((2, 3 * subs - 1)),
+            dma((2, groups - 1)),
+        ],
+        compiler_params=pltpu.CompilerParams(
+            collective_id=0, has_side_effects=True, vmem_limit_bytes=40 * 1024 * 1024
+        ),
+        name="tree_passes",
+    )(
+        positions,
+        far2_list,
+        far3_list,
+        bundle,
+        inverse,
+        basis,
+        transfer1.reshape(clusters, -1, rank),
+        coupling2.reshape(clusters, -1, rank),
+        transfer2.reshape(transfer2.shape[0] // 8, -1, rank),
+        coupling3.reshape(-1, rank),
+    )
+
+
+def classes(points):
+    return points // 2, 3 * points // 4, points
 
 
 def near_kernel(
@@ -92,7 +373,7 @@
         for side in range(2):
             copies.append(
                 pltpu.make_async_copy(
-                    halo_charges.at[lane, side, pl.ds(0, leaf_dev)],
+                    halo_charges.at[side, lane, pl.ds(0, leaf_dev)],
                     charge_table.at[pl.ds(2 * side * group_size + lane * leaf_dev, leaf_dev)],
                     sems.at[4 + 2 * lane + side],
                 )
@@ -114,37 +395,38 @@
     feature_table[dead] = feature_table[group_size]
     charge_table[dead] = jnp.zeros(charge_table.shape[1:], charge_table.dtype)
 
-    def distances(step):
+    def distances(step, rows_used):
         for u in range(ITEMS):
             item = step * ITEMS + u
-            t = jnp.minimum(item_leaf[item], leaf_dev - 1)
+            t = item_leaf[item]
             p = item_start[item]
             rows = [feature_table[near[p + k]] for k in range(SLOTS)]
-            squared[u] = jnp.dot(
-                target_table[t],
+            squared[u, :rows_used] = jnp.dot(
+                target_table[t, :rows_used],
                 jnp.concatenate(rows, axis=1),
                 preferred_element_type=jnp.float32,
             ).astype(jnp.bfloat16)
 
-    def products(step):
+    def products(step, rows_used):
         for u in range(ITEMS):
             item = step * ITEMS + u
-            t = jnp.minimum(item_leaf[item], leaf_dev - 1)
+            t = item_leaf[item]
             p = item_start[item]
             rows = [charge_table[inverse[near[p + k]]] for k in range(SLOTS)]
-            out_ref[t] += lax.dot_general(
+            out_ref[t, :, :rows_used] += lax.dot_general(
                 jnp.concatenate(rows, axis=1),
-                lax.rsqrt(squared[u]),
-                (((1,), (1,)), ((), ())),
+                lax.rsqrt(squared[u, :rows_used]),
+                NT,
                 preferred_element_type=jnp.float32,
             )
 
-    distances(0)
-
-    @pl.loop(1, steps[0] + 1)
-    def _(step):
-        products(step - 1)
-        distances(step)
+    for kind, rows_used in enumerate(classes(out_ref.shape[2])):
+        distances(steps[kind], rows_used)
+
+        @pl.loop(steps[kind] + 1, steps[kind + 1] + 1)
+        def _(step):
+            products(step - 1, rows_used)
+            distances(step, rows_used)
 
     place = lax.broadcasted_iota(jnp.int32, out_ref.shape[1:], 1)
 
@@ -164,15 +446,25 @@
     chunks = -(-slots // SLOTS)
     live = jnp.sum((near >= 0).astype(jnp.int32), axis=1)
     used = (live + SLOTS - 1) // SLOTS
-    ends = jnp.cumsum(used)
-    capacity = leaf_dev * chunks + 2 * ITEMS
-    item = jnp.arange(capacity, dtype=jnp.int32)
-    before = ends[None, :] <= item[:, None]
-    leaf = jnp.sum(before.astype(jnp.int32), axis=1)
-    first = jnp.max(jnp.where(before, ends[None, :], 0), axis=1)
+    limits = classes(points)
+    kind = sum((counts > limit).astype(jnp.int32) for limit in limits[:-1])
+    leaf = jnp.arange(leaf_dev, dtype=jnp.int32)
+    first = jnp.zeros((leaf_dev,), jnp.int32)
+    steps = [jnp.zeros((), jnp.int32)]
+    earlier = leaf[None, :] < leaf[:, None]
+    for k in range(len(limits)):
+        amount = jnp.where(kind == k, used, 0)
+        place = steps[-1] * ITEMS + jnp.sum(jnp.where(earlier, amount[None, :], 0), axis=1)
+        first = jnp.where(kind == k, place, first)
+        steps.append(steps[-1] + (jnp.sum(amount) + ITEMS - 1) // ITEMS)
+    steps = jnp.stack(steps)
+    capacity = leaf_dev * chunks + (len(limits) + 1) * ITEMS
+    item = jnp.arange(capacity, dtype=jnp.int32)[:, None]
     row = chunks * SLOTS
-    start = jnp.where(leaf < leaf_dev, leaf * row + SLOTS * (item - first), leaf_dev * row)
-    steps = ((ends[-1:] + ITEMS - 1) // ITEMS).astype(jnp.int32)
+    chosen = (item >= first[None, :]) & (item < (first + used)[None, :])
+    item_leaf = jnp.sum(jnp.where(chosen, leaf[None, :], 0), axis=1)
+    at = leaf[None, :] * row + SLOTS * (item - first[None, :])
+    start = jnp.sum(jnp.where(chosen, at - leaf_dev * row, 0), axis=1) + leaf_dev * row
     padded = jnp.pad(
         jnp.where(near >= 0, near, dead), ((0, 1), (0, row - slots)), constant_values=dead
     ).reshape(-1)
@@ -195,8 +487,8 @@
         compiler_params=pltpu.CompilerParams(vmem_limit_bytes=48 * 1024 * 1024),
         name="near_field",
     )(
-        leaf.astype(jnp.int32),
-        start.astype(jnp.int32),
+        item_leaf,
+        start,
         steps,
         padded,
         inverse,
@@ -228,73 +520,54 @@
     group = lax.axis_index("leaf")
     subs = lax.axis_size("sub")
     leaf_dev, rhs_count, points = charges.shape
-    rank_size = basis.shape[1]
     group_size = coords.shape[0]
-    clusters = far2_list.shape[0]
-    group_boxes = transfer2.shape[0]
     start = lane * leaf_dev
 
+    groups = lax.axis_size("leaf")
+    number = jnp.arange(group_size, dtype=jnp.int32)
     slot = lax.dynamic_slice_in_dim(morton, start, leaf_dev, 0)
-    arriving_counts = counts[slot]
+    arriving_counts = jnp.sum(
+        jnp.where(slot[:, None] == number[None, :], counts[None, :], 0), axis=1
+    )
     place = jnp.arange(points, dtype=jnp.int32)
     masked = jnp.where(
         place[None, None, :] < arriving_counts[:, None, None], charges, jnp.zeros((), charges.dtype)
     )
-    arrived = lax.all_gather(masked, "sub", axis=0, tiled=True)
     planes = coords.transpose(1, 0, 2)
     own_planes = lax.dynamic_slice_in_dim(planes, start, leaf_dev, 1)
     bundle = jnp.concatenate([masked, own_planes.reshape(-1, rhs_count, points)], axis=0)
-    sides = jnp.stack([shift(bundle, "leaf", 1), shift(bundle, "leaf", -1)])
-    halo = lax.all_gather(sides, "sub", axis=0)
-
-    inverse = (
-        jnp.zeros((group_size,), jnp.int32).at[morton].set(jnp.arange(group_size, dtype=jnp.int32))
-    )
+    inverse = jnp.sum(
+        jnp.where(morton[None, :] == number[:, None], number[None, :], 0), axis=1
+    )
+    own_features = features(planes, False)
+    targets = features(own_planes, True)
+    arrived, halo, halo_inverse, far_part = tree_passes(
+        groups,
+        subs,
+        lax.dynamic_slice_in_dim(inverse, start, leaf_dev, 0),
+        far2_list,
+        far3_list,
+        bundle,
+        inverse.reshape(-1, points),
+        basis,
+        transfer1,
+        coupling2,
+        transfer2,
+        coupling3,
+    )
+    arrived = arrived.reshape(group_size, rhs_count, points)
+    halo_inverse = halo_inverse.reshape(2, group_size)
     all_inverse = jnp.concatenate(
         [
-            shift(inverse, "leaf", 1),
+            halo_inverse[0],
             inverse + group_size,
-            shift(inverse, "leaf", -1) + 2 * group_size,
+            halo_inverse[1] + 2 * group_size,
             jnp.full((1,), 3 * group_size, jnp.int32),
         ]
     )
-    own_features = features(planes, False)
-    targets = features(own_planes, True)
-    halo_planes = halo[:, :, leaf_dev:].reshape(subs, 2, 3, leaf_dev, points)
-    halo_planes = halo_planes.transpose(2, 1, 0, 3, 4).reshape(3, 2 * group_size, points)
+    halo_planes = halo[:, :, leaf_dev:].reshape(2, subs, 3, leaf_dev, points)
+    halo_planes = halo_planes.transpose(2, 0, 1, 3, 4).reshape(3, 2 * group_size, points)
     halo_features = features(halo_planes, False).reshape(2, group_size, FEATURES, points)
-
-    own_charges = arrived[lax.dynamic_slice_in_dim(inverse, start, leaf_dev, 0)]
-    transfer_boxed = transfer1.reshape(clusters, 8, rank_size, rank_size)
-    leaf_moments = jnp.einsum(
-        "trp,tkp->trk", own_charges, basis, preferred_element_type=jnp.float32
-    ).astype(jnp.bfloat16)
-    box_moments = jnp.einsum(
-        "bnrc,bncp->brp",
-        leaf_moments.reshape(clusters, 8, rhs_count, rank_size),
-        transfer_boxed,
-        preferred_element_type=jnp.float32,
-    ).astype(jnp.bfloat16)
-    group_moments = lax.all_gather(box_moments, "sub", axis=0, tiled=True)
-    top_moment = jnp.einsum(
-        "brc,bcp->rp", group_moments, transfer2, preferred_element_type=jnp.float32
-    ).astype(jnp.bfloat16)
-    all_top = lax.all_gather(top_moment[None], "leaf", axis=0, tiled=True)
-    near_boxes = jnp.concatenate(
-        [shift(group_moments, "leaf", 1), group_moments, shift(group_moments, "leaf", -1)], axis=0
-    )
-    top_field = far_field(all_top, far3_list, coupling3, 0).astype(jnp.bfloat16)
-    box_far = far_field(near_boxes, far2_list, coupling2, (group - 1) * group_boxes)
-    own_transfer = lax.dynamic_slice_in_dim(transfer2, lane * clusters, clusters, 0)
-    box_local = (
-        box_far
-        + jnp.einsum("rp,bcp->brc", top_field[0], own_transfer, preferred_element_type=jnp.float32)
-    ).astype(jnp.bfloat16)
-    leaf_local = jnp.einsum(
-        "brp,bncp->bnrc", box_local, transfer_boxed, preferred_element_type=jnp.float32
-    ).astype(jnp.bfloat16)
-    leaf_local = leaf_local.reshape(leaf_dev, rhs_count, rank_size)
-    far_part = jnp.einsum("trk,tkp->trp", leaf_local, basis, preferred_element_type=jnp.float32)
 
     base = (group - 1) * group_size
     near = jnp.where(near_list >= 0, near_list - base, -1)

time: 196 us -> 154 us (0.79)
  the two profiles are of different devices: /device:TPU:4 before, /device:TPU:10 now
where the time goes in v2:
time: 154 us
  Pallas kernels  120 us (78%)
  other arithmetic  16.9 us (11%)
  local copies, waits for them, and re-layouts  14.3 us (9%)
  between operations  2.3 us (1%)
    pallas_call x1, Pallas kernels, near_field(): pl.pallas_call(functools.partial(near_kernel, (leaf_dev, group_size, subs...  69.6 us
    pallas_call x1, Pallas kernels, tree_passes(): pl.pallas_call(functools.partial(tree_kernel, groups, subs), out_shape=(j...  50.6 us
    unnamed x28, local copies, waits for them, and re-layouts  12.3 us
    convert_element_type x3, other arithmetic, features(): return total.astype(jnp.bfloat16)  10.3 us

profile of v2, /device:TPU:10, one launch (start us, length us, event | category | flops | bytes accessed | tf_op | source)
XLA Modules:
  0.0 153.8 jit_solution(6820063236700390426)
XLA Ops:
  0.0 0.8 dynamic_slice.14
  0.8 0.9 select_reduce_fusion.3
  1.6 0.1 iota_compare_fusion.4
  1.7 1.0 broadcast_select_fusion
  2.8 1.0 constant_dynamic-slice_fusion
  3.8 0.9 select_reduce_fusion
  4.8 3.9 %copy.17 = bf16[128,64,64]{2,1,0:T(8,128)(2,1)S(1)} copy(bf16[128,64,64]{0,2,1:T(8,128)(2,1)} %param.18) | data formatting | bytes 2097152 | tf_op args[6]
  8.7 2.2 %copy-done.1 = bf16[16,16,64,64]{3,2,1,0:T(8,128)(2,1)S(1)} copy-done((bf16[16,16,64,64]{3,2,1,0:T(8,128)(2,1)S(1)}, bf16[16,16,64,64]{3,2,1,0:T(8,128)(2,1)}, u32[]{:S(2)}) %copy-start.1) | copy-done | bytes 2097176
  10.9 1.6 %copy-done.2 = bf16[128,64,128]{2,1,0:T(8,128)(2,1)S(1)} copy-done((bf16[128,64,128]{2,1,0:T(8,128)(2,1)S(1)}, bf16[128,64,128]{2,1,0:T(8,128)(2,1)}, u32[]{:S(2)}) %copy-start.2) | copy-done | bytes 2097176
  12.5 0.9 copy-done.8
  13.4 50.6 %tree_passes.1 = (bf16[4,128,8,128]{3,2,1,0:T(8,128)(2,1)S(1)}, bf16[2,4,176,8,128]{4,3,2,1,0:T(8,128)(2,1)S(1)}, s32[2,4,128]{2,1,0:T(4,128)S(1)}, f32[128,8,128]{2,1,0:T(8,128)S(1)}) custom-call(s32[128]{0:T(128)S(1)} %dynamic_slice.13.positions, s32[16,16]{1,0:T(8,128)S(1)} %copy-done.9, s32[1,8]{1,0:T(1,128)S(1)} %copy-done.10, ...), custom_call_target="tpu_custom_call" | custom-call | tf_op jit(solution)/shard_map/tree_passes/pallas_call | solution.py:292
  64.1 0.8 copy-done.6
  64.9 0.1 fusion.1
  65.1 0.1 fusion.9
  65.2 1.2 copy-done
  66.5 0.3 copy-done.4
  66.7 0.2 convert_multiply_fusion
  67.0 6.5 %select_convert_fusion.halo_features = bf16[2,512,16,128]{3,2,1,0:T(8,128)(2,1)} fusion(bf16[2,512,128]{2,1,0:T(8,128)(2,1)S(1)} %bitcast.104, bf16[2,512,128]{2,1,0:T(8,128)(2,1)S(1)} %bitcast.103, bf16[2,512,128]{2,1,0:T(8,128)(2,1)S(1)} %bitcast.102, bf16[2,512,128]{2,1,0:T(8,128)(2,1)S(1)} %get-tuple-element.32, ...), kind=kLoop, calls=%fused_computation | loop fusion | flops 18874368 | bytes 5767312 | tf_op jit(solution)/shard_map/convert_element_type | solution.py:39
  73.5 1.5 fusion.21
  75.6 0.7 fusion.23
  77.7 0.1 select_reduce_fusion.4
  77.8 0.1 select_reduce_fusion.6
  78.0 0.4 select_reduce_fusion.1
  78.5 0.9 select_convert_fusion.2.target_ref
  79.4 0.1 reduce-precision_subtract_fusion
  79.6 0.1 fusion.19
  79.7 0.1 fusion.8
  79.8 2.9 %select_convert_fusion.1.own_features = bf16[512,16,128]{2,1,0:T(8,128)(2,1)S(1)} fusion(bf16[512,128]{1,0:T(8,128)(2,1)S(1)} %get-tuple-element.35, bf16[512,128]{1,0:T(8,128)(2,1)S(1)} %get-tuple-element.34, bf16[512,128]{1,0:T(8,128)(2,1)S(1)} %get-tuple-element.33, f32[512,128]{1,0:T(8,128)S(1)} %get-tuple-element.16, bf16[512,128]{1,0:T(8,128)(2,1)S(1)} %fusion.19, ...), kind=kLoop, calls=%fused_computation.1 | loop fusion | flops 9437184 | bytes 3014800 | tf_op jit(solution)/shard_map/convert_element_type | solution.py:39
  82.7 0.1 copy.18
  82.8 0.1 reshape.330.near
  82.9 1.2 copy-done.5
  84.1 69.6 %near_field.1 = f32[128,8,128]{2,1,0:T(8,128)} custom-call(s32[912]{0:T(1024)S(1)} %get-tuple-element.14.item_leaf, s32[912]{0:T(1024)S(1)} %broadcast_add_fusion.item_start, s32[4]{0:T(128)S(1)} %pad_add_fusion.1.steps, s32[3612]{0:T(1024)S(1)} %reshape.330.near, s32[1537]{0:T(1024)S(1)} %pad_add_fusion.inverse, s32[128]{0:T(128)S(1)} %get-tuple-element.19.counts, ...), custom_call_target="tpu_custom_call" | custom-call | tf_op jit(solution)/shard_map/near_field/pallas_call | solution.py:475
  (39 shorter events, 0.5 us)
Async XLA Ops:
  2.7 6.0 %copy-start.3 = (bf16[64,64,64]{2,1,0:T(8,128)(2,1)S(1)}, bf16[64,64,64]{2,1,0:T(8,128)(2,1)}, u32[]{:S(2)}) copy-start(bf16[64,64,64]{2,1,0:T(8,128)(2,1)} %param.21) | copy-start | bytes 1572868
  2.8 6.0 %copy-start.9 = (s32[16,16]{1,0:T(8,128)S(1)}, s32[16,16]{1,0:T(8,128)}, u32[]{:S(2)}) copy-start(s32[16,16]{1,0:T(8,128)} %far2.1) | copy-start | bytes 3076
  2.8 6.0 %copy-start.10 = (s32[1,8]{1,0:T(1,128)S(1)}, s32[1,8]{1,0:T(1,128)}, u32[]{:S(2)}) copy-start(s32[1,8]{1,0:T(1,128)} %far3.1) | copy-start | bytes 100
  8.7 2.2 %copy-start.1 = (bf16[16,16,64,64]{3,2,1,0:T(8,128)(2,1)S(1)}, bf16[16,16,64,64]{3,2,1,0:T(8,128)(2,1)}, u32[]{:S(2)}) copy-start(bf16[16,16,64,64]{3,2,1,0:T(8,128)(2,1)} %param.20) | copy-start | bytes 6291460
  10.9 1.6 %copy-start.2 = (bf16[128,64,128]{2,1,0:T(8,128)(2,1)S(1)}, bf16[128,64,128]{2,1,0:T(8,128)(2,1)}, u32[]{:S(2)}) copy-start(bf16[128,64,128]{2,1,0:T(8,128)(2,1)} %basis.1) | copy-start | bytes 6291460
  12.5 0.9 copy-start.8
  64.1 0.8 copy-start.6
  64.9 1.6 %copy-start = (bf16[2,4,176,8,128]{4,3,2,1,0:T(8,128)(2,1)}, bf16[2,4,176,8,128]{4,3,2,1,0:T(8,128)(2,1)S(1)}, u32[]{:S(2)}) copy-start(bf16[2,4,176,8,128]{4,3,2,1,0:T(8,128)(2,1)S(1)} %get-tuple-element.10.halo_charges) | copy-start | bytes 8650756
  64.9 1.9 %copy-start.4 = (bf16[4,128,8,128]{3,2,1,0:T(8,128)(2,1)}, bf16[4,128,8,128]{3,2,1,0:T(8,128)(2,1)S(1)}, u32[]{:S(2)}) copy-start(bf16[4,128,8,128]{3,2,1,0:T(8,128)(2,1)S(1)} %get-tuple-element.11) | copy-start | bytes 3145732
  67.0 6.5 %copy-start.12 = (s32[128,27]{0,1:T(8,128)S(1)}, s32[128,27]{0,1:T(8,128)}, u32[]{:S(2)}) copy-start(s32[128,27]{0,1:T(8,128)} %param.16) | copy-start | bytes 41476
  67.0 11.4 %copy-start.11 = (bf16[512,3,128]{2,0,1:T(8,128)(2,1)S(1)}, bf16[512,3,128]{2,0,1:T(8,128)(2,1)}, u32[]{:S(2)}) copy-start(bf16[512,3,128]{2,0,1:T(8,128)(2,1)} %param.12) | copy-start | bytes 1179652
  79.7 3.2 %copy-start.7 = (f32[128,8,128]{2,1,0:T(8,128)S(1)}, f32[128,8,128]{2,1,0:T(8,128)}, u32[]{:S(2)}) copy-start(f32[128,8,128]{2,1,0:T(8,128)} %copy-done.6) | copy-start | bytes 1572868
  82.9 1.2 copy-start.5

commit v3 on v2

--- a/solution.py
+++ b/solution.py
@@ -10,7 +10,8 @@
 kernel_scale = 0.07957747154594767
 delta_squared = 0.0025
 SLOTS = 4
-ITEMS = 4
+ITEMS = 8
+CHUNKS = 4
 FEATURES = 16
 
 
@@ -18,25 +19,30 @@
 
 
 def pieces(value):
-    high = lax.reduce_precision(value, 8, 7)
+    high = value.astype(jnp.bfloat16).astype(jnp.float32)
     rest = value - high
-    middle = lax.reduce_precision(rest, 8, 7)
+    middle = rest.astype(jnp.bfloat16).astype(jnp.float32)
     return high, middle, rest - middle
 
 
-def features(planes, target):
-    x, y, z = (planes[i].astype(jnp.float32) for i in range(3))
+def placement():
+    row = lax.broadcasted_iota(jnp.int32, (8 * FEATURES, 72), 0)
+    column = lax.broadcasted_iota(jnp.int32, (8 * FEATURES, 72), 1)
+    same = (row // FEATURES == column % 8) & (row % FEATURES == column // 8)
+    return jnp.where(same, 1.0, 0.0).astype(jnp.bfloat16)
+
+
+def features(place, planes, target):
+    x, y, z = (plane.astype(jnp.float32) for plane in planes)
     norm = x * x + y * y + z * z
     one = jnp.ones_like(x)
     if target:
         rows = [x, y, z, *pieces(norm + delta_squared), one, one, one]
     else:
         rows = [-2.0 * x, -2.0 * y, -2.0 * z, one, one, one, *pieces(norm)]
-    place = lax.broadcasted_iota(jnp.int32, (1, FEATURES, 1), 1)
-    total = jnp.zeros((x.shape[0], FEATURES, x.shape[1]), jnp.float32)
-    for k, row in enumerate(rows):
-        total = jnp.where(place == k, row[:, None, :], total)
-    return total.astype(jnp.bfloat16)
+    stacked = jnp.concatenate(rows, axis=0).astype(jnp.bfloat16)
+    placed = jnp.dot(place, stacked, preferred_element_type=jnp.float32)
+    return placed.reshape(8, FEATURES, x.shape[1])
 
 
 NT = (((1,), (1,)), ((), ()))
@@ -58,15 +64,20 @@
     far3,
     bundle,
     inverse,
+    basis_in,
+    transfer1_in,
+    coupling2_in,
+    transfer2_in,
+    coupling3_in,
+    own_table,
+    halo,
+    halo_inverse,
+    far_ref,
     basis,
     transfer1,
     coupling2,
     transfer2,
     coupling3,
-    own_table,
-    halo,
-    halo_inverse,
-    far_ref,
     boxes,
     tops,
     box_far,
@@ -97,7 +108,16 @@
         pl.semaphore_signal(barrier, inc=1, device_id=peer, device_id_type=MESH)
     pl.semaphore_wait(barrier, len(peers))
 
-    def send(source, target, sems, index, device):
+    def run(when, action):
+        if when is None:
+            action()
+        else:
+
+            @pl.when(when)
+            def _():
+                action()
+
+    def send(source, target, sems, index, device, when=None):
         copy = pltpu.make_async_remote_copy(
             src_ref=source,
             dst_ref=target,
@@ -106,10 +126,22 @@
             device_id=device,
             device_id_type=MESH,
         )
-        copy.start()
-        return copy
+        run(when, copy.start)
+        return when, copy
 
     started = []
+    weights = [
+        pltpu.make_async_copy(source, target, local_sems.at[1 + k])
+        for k, (source, target) in enumerate(
+            [
+                (basis_in, basis),
+                (transfer1_in, transfer1),
+                (transfer2_in, transfer2),
+                (coupling2_in, coupling2),
+                (coupling3_in, coupling3),
+            ]
+        )
+    ]
     bits = []
     bit = subs // 2
     while bit:
@@ -120,20 +152,38 @@
     keep = [
         pltpu.make_async_copy(charges, own_table.at[lane], local_sems.at[0]),
     ]
-    for copy in keep:
+    for copy in keep + weights:
         copy.start()
     first = send(charges, own_table.at[lane], own_sems, 0, (group, flip(lane, bits[0])))
     started.append(first)
-    sides = [
-        send(bundle, halo.at[0, lane], side_sems, 0, (after, lane)),
-        send(bundle, halo.at[1, lane], side_sems, 1, (before, lane)),
+    inverses = [
         send(inverse, halo_inverse.at[0], inverse_sems, 0, (after, lane)),
         send(inverse, halo_inverse.at[1], inverse_sems, 1, (before, lane)),
     ]
-    started += sides
+    started += inverses
+    part = bundle.shape[0] // CHUNKS
+    has_before = group > 0
+    has_after = group < groups - 1
+    filled = [has_before, has_after]
+    arrivals = []
+    for chunk in range(CHUNKS):
+        span = pl.ds(chunk * part, part)
+        pair = [
+            send(
+                bundle.at[span],
+                halo.at[side, lane, span],
+                side_sems,
+                2 * chunk + side,
+                ((after, before)[side], lane),
+                (has_after, has_before)[side],
+            )
+            for side in range(2)
+        ]
+        started += pair
+        arrivals.append(pair)
     for copy in keep:
         copy.wait()
-    first.wait_recv()
+    first[1].wait_recv()
     held = [lane, flip(lane, bits[0])]
     count = 1
     for bit in bits[1:]:
@@ -150,10 +200,37 @@
             )
             count += 1
         started += copies
-        for copy in copies:
+        for _, copy in copies:
             copy.wait_recv()
         held = held + [flip(block, bit) for block in held]
 
+    def forward(bit, held, chunk, stage):
+        span = pl.ds(chunk * part, part)
+        copies = []
+        for k, block in enumerate(held):
+            for side in range(2):
+                copies.append(
+                    send(
+                        halo.at[side, block, span],
+                        halo.at[side, block, span],
+                        halo_sems,
+                        2 * (chunk * (subs - 1) + stage + k) + side,
+                        (group, flip(lane, bit)),
+                        filled[side],
+                    )
+                )
+        return copies
+
+    def received(chunk, copies):
+        for side, (_, copy) in zip([0, 1] * len(copies), copies):
+            run(filled[side], copy.wait_recv)
+
+    passed = []
+    for chunk in range(CHUNKS // 2):
+        received(chunk, arrivals[chunk])
+        passed.append(forward(bits[0], [lane], chunk, 0))
+    for copy in weights[:2]:
+        copy.wait()
     mine = boxes.at[1, lane]
 
     @pl.loop(0, clusters)
@@ -180,32 +257,15 @@
     started += copies
     box_copies = copies
 
-    for copy in sides:
-        copy.wait_recv()
-    held = [lane]
-    count = 0
-    halo_copies = []
-
-    def forward(bit, held, count):
-        copies = []
-        for block in held:
-            for side in range(2):
-                copies.append(
-                    send(
-                        halo.at[side, block],
-                        halo.at[side, block],
-                        halo_sems,
-                        count,
-                        (group, flip(lane, bit)),
-                    )
-                )
-                count += 1
-        return copies, held + [flip(block, bit) for block in held], count
-
-    halo_copies, held, count = forward(bits[0], held, count)
-    started += halo_copies
-
-    for copy in box_copies:
+    for chunk in range(CHUNKS // 2, CHUNKS):
+        received(chunk, arrivals[chunk])
+        passed.append(forward(bits[0], [lane], chunk, 0))
+    for copies in passed:
+        started += copies
+
+    for copy in weights[2:]:
+        copy.wait()
+    for _, copy in box_copies:
         copy.wait_recv()
 
     def top_step(chunk, total):
@@ -234,13 +294,19 @@
             cells.append(jnp.where(name >= 0, cell, jnp.zeros_like(cell)))
         box_far[b] = matmul(jnp.concatenate(cells, axis=1), coupling2[b])
 
+    held = [lane, flip(lane, bits[0])]
+    stage = 1
     for bit in bits[1:]:
-        for copy in halo_copies:
-            copy.wait_recv()
-        halo_copies, held, count = forward(bit, held, count)
-        started += halo_copies
-
-    for copy in top_copies:
+        later = []
+        for chunk in range(CHUNKS):
+            received(chunk, passed[chunk])
+            later.append(forward(bit, held, chunk, stage))
+            started += later[-1]
+        stage += len(held)
+        held = held + [flip(block, bit) for block in held]
+        passed = later
+
+    for _, copy in top_copies:
         copy.wait_recv()
     cells = []
     for k in range(slots3):
@@ -262,10 +328,12 @@
         for u in range(8):
             far_ref[b * 8 + u] = matmul(leaves[:, u * rank : (u + 1) * rank], basis[b * 8 + u])
 
-    for copy in halo_copies:
+    for chunk in range(CHUNKS):
+        received(chunk, passed[chunk])
+    for _, copy in inverses:
         copy.wait_recv()
-    for copy in started:
-        copy.wait_send()
+    for when, copy in started:
+        run(when, copy.wait_send)
 
 
 def tree_passes(
@@ -297,22 +365,27 @@
             jax.ShapeDtypeStruct((2,) + inverse.shape, jnp.int32),
             jax.ShapeDtypeStruct((leaf_dev, rhs, points), jnp.float32),
         ),
-        in_specs=[smem] * 3 + [hbm] * 2 + [vmem] * 5,
+        in_specs=[smem] * 3 + [hbm] * 7,
         out_specs=(vmem, hbm, hbm, vmem),
         scratch_shapes=[
+            pltpu.VMEM(basis.shape, jnp.bfloat16),
+            pltpu.VMEM((clusters, 8 * rank, rank), jnp.bfloat16),
+            pltpu.VMEM((clusters, far2_list.shape[1] * rank, rank), jnp.bfloat16),
+            pltpu.VMEM((transfer2.shape[0] // 8, 8 * rank, rank), jnp.bfloat16),
+            pltpu.VMEM((far3_list.shape[1] * rank, rank), jnp.bfloat16),
             pltpu.VMEM((3, subs, clusters, rhs, rank), jnp.bfloat16),
             pltpu.VMEM((groups, rhs, rank), jnp.bfloat16),
             pltpu.VMEM((clusters, rhs, rank), jnp.float32),
-            dma((1,)),
+            dma((6,)),
             dma((2, subs - 1)),
+            dma((2, 2 * CHUNKS)),
             dma((2, 2)),
-            dma((2, 2)),
-            dma((2, 2 * (subs - 1))),
+            dma((2, 2 * CHUNKS * (subs - 1))),
             dma((2, 3 * subs - 1)),
             dma((2, groups - 1)),
         ],
         compiler_params=pltpu.CompilerParams(
-            collective_id=0, has_side_effects=True, vmem_limit_bytes=40 * 1024 * 1024
+            collective_id=0, has_side_effects=True, vmem_limit_bytes=56 * 1024 * 1024
         ),
         name="tree_passes",
     )(
@@ -341,54 +414,79 @@
     near,
     inverse,
     counts,
-    target_ref,
-    own_features,
-    halo_features,
+    target_planes,
+    own_planes,
     own_charges,
-    halo_charges,
+    halo,
     far_ref,
     out_ref,
     feature_table,
     charge_table,
     target_table,
+    halo_planes,
     squared,
     sems,
 ):
     leaf_dev, group_size, subs = sizes
+    blocks = leaf_dev // 8
+    plane_copies = [
+        pltpu.make_async_copy(
+            halo.at[side, lane, pl.ds(leaf_dev, 3 * blocks)],
+            halo_planes.at[side, lane],
+            sems.at[1, 2 * lane + side],
+        )
+        for lane in range(subs)
+        for side in range(2)
+    ]
     copies = [
         pltpu.make_async_copy(
-            own_features, feature_table.at[pl.ds(group_size, group_size)], sems.at[0]
-        ),
-        pltpu.make_async_copy(
-            halo_features.at[0], feature_table.at[pl.ds(0, group_size)], sems.at[1]
-        ),
-        pltpu.make_async_copy(
-            halo_features.at[1], feature_table.at[pl.ds(2 * group_size, group_size)], sems.at[2]
-        ),
-        pltpu.make_async_copy(
-            own_charges, charge_table.at[pl.ds(group_size, group_size)], sems.at[3]
-        ),
+            own_charges, charge_table.at[pl.ds(group_size, group_size)], sems.at[0, 2 * subs]
+        )
     ]
     for lane in range(subs):
         for side in range(2):
             copies.append(
                 pltpu.make_async_copy(
-                    halo_charges.at[side, lane, pl.ds(0, leaf_dev)],
+                    halo.at[side, lane, pl.ds(0, leaf_dev)],
                     charge_table.at[pl.ds(2 * side * group_size + lane * leaf_dev, leaf_dev)],
-                    sems.at[4 + 2 * lane + side],
+                    sems.at[0, 2 * lane + side],
                 )
             )
-    for copy in copies:
+    for copy in plane_copies + copies:
         copy.start()
-
-    @pl.loop(0, leaf_dev // 8)
+    place = placement()
+
+    @pl.loop(0, blocks // 2)
+    def _(pair):
+        for v in range(2):
+            block = pair * 2 + v
+            built = features(place, [target_planes[c * blocks + block] for c in range(3)], True)
+            for u in range(8):
+                target_table[block * 8 + u] = built[u].T.astype(jnp.bfloat16)
+
+    @pl.loop(0, subs * blocks // 4)
+    def _(four):
+        for v in range(4):
+            block = four * 4 + v
+            built = features(
+                place, [own_planes[c * subs * blocks + block] for c in range(3)], False
+            )
+            feature_table[pl.ds(group_size + block * 8, 8)] = built.astype(jnp.bfloat16)
+
+    out_ref[...] = jnp.zeros_like(out_ref)
+    for copy in plane_copies:
+        copy.wait()
+
+    @pl.loop(0, blocks)
     def _(block):
-        for u in range(8):
-            t = block * 8 + u
-            turned = target_ref[t].astype(jnp.float32).T
-            target_table[t] = turned.astype(jnp.bfloat16)
-
-    out_ref[...] = jnp.zeros_like(out_ref)
+        for lane in range(subs):
+            for side in range(2):
+                built = features(
+                    place, [halo_planes[side, lane, c * blocks + block] for c in range(3)], False
+                )
+                begin = 2 * side * group_size + lane * leaf_dev + block * 8
+                feature_table[pl.ds(begin, 8)] = built.astype(jnp.bfloat16)
+
     for copy in copies:
         copy.wait()
     dead = 3 * group_size
@@ -438,9 +536,9 @@
             out_ref[t] = jnp.where(place < counts[t], total, 0.0)
 
 
-def near_field(targets, own, halo, own_charges, halo_charges, near, inverse, counts, far, subs):
+def near_field(targets, own, own_charges, halo, near, inverse, counts, far, subs):
     leaf_dev, slots = near.shape
-    group_size = own.shape[0]
+    group_size = own_charges.shape[0]
     points = own.shape[2]
     dead = 3 * group_size
     chunks = -(-slots // SLOTS)
@@ -475,14 +573,15 @@
     return pl.pallas_call(
         functools.partial(near_kernel, (leaf_dev, group_size, subs)),
         out_shape=jax.ShapeDtypeStruct((leaf_dev, rhs, points), jnp.float32),
-        in_specs=[smem] * 6 + [vmem, hbm, hbm, hbm, hbm, vmem],
+        in_specs=[smem] * 6 + [vmem, vmem, hbm, hbm, vmem],
         out_specs=vmem,
         scratch_shapes=[
             pltpu.VMEM((dead + 1, FEATURES, points), jnp.bfloat16),
             pltpu.VMEM((dead + 1, rhs, points), jnp.bfloat16),
             pltpu.VMEM((leaf_dev, points, FEATURES), jnp.bfloat16),
+            pltpu.VMEM((2, subs, 3 * leaf_dev // 8, 8, points), jnp.bfloat16),
             pltpu.VMEM((ITEMS, points, SLOTS * points), jnp.bfloat16),
-            pltpu.SemaphoreType.DMA((4 + 2 * subs,)),
+            pltpu.SemaphoreType.DMA((2, 2 * subs + 1)),
         ],
         compiler_params=pltpu.CompilerParams(vmem_limit_bytes=48 * 1024 * 1024),
         name="near_field",
@@ -495,9 +594,8 @@
         counts,
         targets,
         own,
+        own_charges,
         halo,
-        own_charges,
-        halo_charges,
         far,
     )
 
@@ -535,12 +633,10 @@
     )
     planes = coords.transpose(1, 0, 2)
     own_planes = lax.dynamic_slice_in_dim(planes, start, leaf_dev, 1)
-    bundle = jnp.concatenate([masked, own_planes.reshape(-1, rhs_count, points)], axis=0)
+    bundle = jnp.concatenate([masked, own_planes.reshape(-1, 8, points)], axis=0)
     inverse = jnp.sum(
         jnp.where(morton[None, :] == number[:, None], number[None, :], 0), axis=1
     )
-    own_features = features(planes, False)
-    targets = features(own_planes, True)
     arrived, halo, halo_inverse, far_part = tree_passes(
         groups,
         subs,
@@ -565,17 +661,12 @@
             jnp.full((1,), 3 * group_size, jnp.int32),
         ]
     )
-    halo_planes = halo[:, :, leaf_dev:].reshape(2, subs, 3, leaf_dev, points)
-    halo_planes = halo_planes.transpose(2, 0, 1, 3, 4).reshape(3, 2 * group_size, points)
-    halo_features = features(halo_planes, False).reshape(2, group_size, FEATURES, points)
-
     base = (group - 1) * group_size
     near = jnp.where(near_list >= 0, near_list - base, -1)
     own_counts = lax.dynamic_slice_in_dim(counts, start, leaf_dev, 0)
     return near_field(
-        targets,
-        own_features,
-        halo_features,
+        own_planes.reshape(-1, 8, points),
+        planes.reshape(-1, 8, points),
         arrived,
         halo,
         near,

time: 154 us -> 136 us (0.88)
  other arithmetic: 16.9 us -> 8.53 us
  Pallas kernels: 120 us -> 113 us
  local copies, waits for them, and re-layouts: 14.3 us -> 11.2 us
    convert_element_type x3 -> x0, other arithmetic: 10.3 us -> none  [features(): return total.astype(jnp.bfloat16)]
    pallas_call x1, Pallas kernels: 69.6 us -> 65.3 us  [near_field(): pl.pallas_call(functools.partial(near_kernel, (leaf_dev, group_size, subs...]
    unnamed x28 -> x12, local copies, waits for them, and re-layouts: 12.3 us -> 8.85 us
    pallas_call x1, Pallas kernels: 50.6 us -> 47.9 us  [tree_passes(): pl.pallas_call(functools.partial(tree_kernel, groups, subs), out_shape=(j...]
where the time goes in v3:
time: 136 us; the launch traced here: 135 us
  Pallas kernels  113 us (83%)
  local copies, waits for them, and re-layouts  11.2 us (8%)
  other arithmetic  8.53 us (6%)
  between operations  2.09 us (2%)
    pallas_call x1, Pallas kernels, near_field(): pl.pallas_call(functools.partial(near_kernel, (leaf_dev, group_size, subs...  65.3 us
    pallas_call x1, Pallas kernels, tree_passes(): pl.pallas_call(functools.partial(tree_kernel, groups, subs), out_shape=(j...  47.9 us
    unnamed x12, local copies, waits for them, and re-layouts  8.85 us

profile of v3, /device:TPU:10, one launch (start us, length us, event | category | flops | bytes accessed | tf_op | source)
XLA Modules:
  0.0 135.1 jit_solution(2635837404045577723)
XLA Ops:
  0.0 0.7 compare_select_fusion
  0.7 1.4 %fusion.3 = (s32[]{:T(128)}, s32[128]{0:T(128)S(1)}, s32[128]{0:T(128)S(1)}, s32[128]{0:T(128)S(1)}) fusion(s32[512]{0:T(512)} %param.14, s32[]{:T(128)S(6)} %select_n.78, s32[128]{0:T(128)S(1)} %get-tuple-element.26), kind=kLoop, calls=%fused_computation.41 | loop fusion | flops 3071 | bytes 2568 | tf_op jit(solution)/shard_map/reduce_sum | solution.py:557
  2.1 0.7 fusion.5
  2.8 0.1 select_reduce_fusion.4
  3.6 0.1 select_reduce_fusion.6
  4.4 0.4 select_reduce_fusion.1
  5.5 0.1 pad_add_fusion.1.steps
  5.6 0.1 copy.18
  5.7 0.1 reshape.69.near
  5.8 0.9 select_reduce_fusion
  6.7 0.0 copy-start.4
  6.7 0.6 dynamic_slice.13.positions
  7.3 0.9 constant_dynamic-slice_fusion
  8.2 0.8 dynamic_slice.14
  8.9 0.9 select_reduce_fusion.3
  9.8 0.1 iota_compare_fusion.4
  9.9 1.0 broadcast_select_fusion
  10.9 0.8 pad_maximum_fusion.bundle
  11.7 4.7 %copy.17 = bf16[128,64,64]{2,1,0:T(8,128)(2,1)} copy(bf16[128,64,64]{0,2,1:T(8,128)(2,1)} %param.18) | data formatting | bytes 2097152 | tf_op args[6]
  16.4 0.0 copy-done.4
  16.4 0.0 copy-start.2
  16.4 47.9 %tree_passes.1 = (bf16[4,128,8,128]{3,2,1,0:T(8,128)(2,1)}, bf16[2,4,176,8,128]{4,3,2,1,0:T(8,128)(2,1)}, s32[2,4,128]{2,1,0:T(4,128)}, f32[128,8,128]{2,1,0:T(8,128)}) custom-call(s32[128]{0:T(128)} %dynamic_slice.13.positions, s32[16,16]{1,0:T(8,128)} %far2.1, s32[1,8]{1,0:T(1,128)} %far3.1, bf16[176,8,128]{2,1,0:T(8,128)(2,1)} %pad_maximum_fusion.bundle, ...), custom_call_target="tpu_custom_call" | custom-call | tf_op jit(solution)/shard_map/tree_passes/pallas_call | solution.py:360
  64.3 0.7 slice_bitcast_fusion
  65.0 0.7 broadcast_add_fusion.1
  65.7 0.0 copy-done.2
  65.7 0.0 copy-start
  65.7 1.8 %copy-done = bf16[2,4,176,8,128]{4,3,2,1,0:T(8,128)(2,1)S(1)} copy-done((bf16[2,4,176,8,128]{4,3,2,1,0:T(8,128)(2,1)S(1)}, bf16[2,4,176,8,128]{4,3,2,1,0:T(8,128)(2,1)}, u32[]{:S(2)}) %copy-start) | copy-done | bytes 2883608
  67.5 0.0 copy-start.1
  67.5 1.2 copy-done.1
  68.7 0.0 copy-start.3
  68.7 1.0 copy-done.3
  69.8 65.3 %near_field.1 = f32[128,8,128]{2,1,0:T(8,128)} custom-call(s32[928]{0:T(1024)S(1)} %get-tuple-element.14.item_leaf, s32[928]{0:T(1024)S(1)} %broadcast_add_fusion.item_start, s32[4]{0:T(128)S(1)} %pad_add_fusion.1.steps, s32[3612]{0:T(1024)S(1)} %reshape.69.near, s32[1537]{0:T(1024)S(1)} %pad_add_fusion.inverse, s32[128]{0:T(128)S(1)} %get-tuple-element.17.counts, ...), custom_call_target="tpu_custom_call" | custom-call | tf_op jit(solution)/shard_map/near_field/pallas_call | solution.py:573
  (5 shorter events, 0.0 us)
Async XLA Ops:
  6.7 9.7 %copy-start.4 = (s32[512]{0:T(512)}, s32[512]{0:T(512)S(1)}, u32[]{:S(2)}) copy-start(s32[512]{0:T(512)S(1)} %select_reduce_fusion) | copy-start | bytes 6148
  16.4 49.3 %copy-start.2 = (bf16[512,3,128]{2,0,1:T(8,128)(2,1)S(1)}, bf16[512,3,128]{2,0,1:T(8,128)(2,1)}, u32[]{:S(2)}) copy-start(bf16[512,3,128]{2,0,1:T(8,128)(2,1)} %param.12) | copy-start | bytes 1179652
  65.7 1.8 %copy-start = (bf16[2,4,176,8,128]{4,3,2,1,0:T(8,128)(2,1)S(1)}, bf16[2,4,176,8,128]{4,3,2,1,0:T(8,128)(2,1)}, u32[]{:S(2)}) copy-start(bf16[2,4,176,8,128]{4,3,2,1,0:T(8,128)(2,1)} %get-tuple-element.11.halo) | copy-start | bytes 8650756
  67.5 1.2 copy-start.1
  68.7 1.0 copy-start.3
